TPU v7x, 128 devices: a whole 4x4x4 slice. The times are simulated.
128 devices in a mesh: row: 16 (over y, x), col: 8 (over z, core).
Axes of the slice: x: 4, y: 4, z: 4, core: 2. Of those that a mesh axis runs over, the one named last changes fastest.
Arguments:
- queries: bfloat16 [2048, 64, 128], P(('row', 'col')), may hold values from -1.75 to 1.75
- passages: bfloat16 [16384, 192, 128], P(('row', 'col')), may hold values from -1.75 to 1.75
- pass_len: int32 [16384], P(('row', 'col')), may hold values from 48 to 192
- send_cont: int32 [128, 128, 4], P(('row', 'col')), may hold values from 0 to 15, as said below
- send_count: int32 [128, 128], P(('row', 'col')), may hold values from 0 to 4, as said below
- cand: int32 [128, 128, 4, 4], P(('row', 'col')), may hold values from 0 to 127
- cand_count: int32 [128, 128, 4], P(('row', 'col')), may hold values from 1 to 4
Outputs:
- scores: float32 [128, 128, 4, 4], P(('row', 'col'))
- best: float32 [2048], P(('row', 'col'))
Inputs may be any that keep to these rules, and one draw needn't show every extreme that they name: The 4 entries of send_cont[s, o, :] are distinct. `send_count`: in every draw some owner receives 4 used slots from every device.
All inputs are finite; a program needn't handle non-finite values.
Results may differ from a plain program's by a relative error of at most 0.0003.
Values may be sent and summed in bfloat16 or wider, within the bound.
No kernel may reach another device: no remote copies, remote signals or barrier semaphores. Data moves between devices by JAX's collectives and lax.ppermute only.
A program may use at most 128 MiB of HBM per device.

v0:
```python
import math

import jax
import jax.numpy as jnp
from jax import lax
from jax.sharding import PartitionSpec as P


def score_items(passages, pass_len, sent_rows, sent_ids):
    leading = sent_rows.shape[:2]
    total = leading[0] * leading[1]
    per_block = math.gcd(total, 64)
    row_blocks = sent_rows.reshape((total // per_block, per_block) + sent_rows.shape[2:])
    id_blocks = sent_ids.reshape((total // per_block, per_block) + sent_ids.shape[2:])
    owned = passages.shape[0]
    tok_slots = passages.shape[1]
    width = passages.shape[2]
    flat_pass = passages.reshape(owned, tok_slots * width)
    owned_iota = jnp.arange(owned, dtype=jnp.int32)

    def one_block(pieces):
        query_rows, cand_rows = pieces
        equal = cand_rows[:, :, None] == owned_iota[None, None, :]
        selector = equal.astype(jnp.bfloat16)
        picked = jnp.einsum("gcn,nf->gcf", selector, flat_pass, preferred_element_type=jnp.float32)
        passage_rows = picked.astype(jnp.bfloat16).reshape(cand_rows.shape + (tok_slots, width))
        lengths = jnp.sum(jnp.where(equal, pass_len[None, None, :], 0), axis=2)
        similar = jnp.einsum(
            "gqd,gcpd->gcqp", query_rows, passage_rows, preferred_element_type=jnp.float32
        )
        inside = lax.broadcasted_iota(jnp.int32, similar.shape, 3) < lengths[:, :, None, None]
        column_max = jnp.max(jnp.where(inside, similar, -jnp.inf), axis=3)
        return jnp.mean(column_max, axis=2)

    results = lax.map(one_block, (row_blocks, id_blocks))
    return results.reshape(leading + (sent_ids.shape[2],))


def body(queries, passages, pass_len, send_cont, send_count, cand, cand_count):
    slot_list = send_cont[0]
    cand_ids = cand[0]
    conts_here = queries.shape[0]
    cont_iota = jnp.arange(conts_here, dtype=jnp.int32)
    pick_table = (slot_list[:, :, None] == cont_iota[None, None, :]).astype(jnp.bfloat16)
    flat_queries = queries.reshape(conts_here, queries.shape[1] * queries.shape[2])
    outgoing = jnp.einsum(
        "osq,qf->osf", pick_table, flat_queries, preferred_element_type=jnp.float32
    )
    outgoing = outgoing.astype(jnp.bfloat16).reshape(slot_list.shape + queries.shape[1:])
    handled = score_items(
        passages,
        pass_len,
        lax.all_to_all(outgoing, ("row", "col"), split_axis=0, concat_axis=0, tiled=True),
        lax.all_to_all(cand_ids, ("row", "col"), split_axis=0, concat_axis=0, tiled=True),
    )
    returned = lax.all_to_all(handled, ("row", "col"), split_axis=0, concat_axis=0, tiled=True)
    slots_here = slot_list.shape[1]
    cands_here = cand_ids.shape[2]
    slot_live = jnp.arange(slots_here, dtype=jnp.int32)[None, :] < send_count[0][:, None]
    cand_live = jnp.arange(cands_here, dtype=jnp.int32)[None, None, :] < cand_count[0][:, :, None]
    live = slot_live[:, :, None] & cand_live
    scores = jnp.where(live, returned, jnp.float32(0.0))
    matches = slot_list[:, :, None] == cont_iota[None, None, :]
    usable = live[:, :, :, None] & matches[:, :, None, :]
    masked = jnp.where(usable, scores[:, :, :, None], -jnp.inf)
    best = jnp.max(masked, axis=(0, 1, 2))
    present = jnp.any(usable, axis=(0, 1, 2))
    best = jnp.where(present, best, jnp.float32(0.0))
    return (scores[None], best)


def solution(mesh):
    in_specs = (
        P(("row", "col"), None, None),
        P(("row", "col"), None, None),
        P(("row", "col")),
        P(("row", "col"), None, None),
        P(("row", "col"), None),
        P(("row", "col"), None, None, None),
        P(("row", "col"), None, None),
    )
    out_specs = (P(("row", "col"), None, None, None), P(("row", "col")))
    return jax.shard_map(body, mesh=mesh, in_specs=in_specs, out_specs=out_specs, check_vma=False)
```

profile of v0, /device:TPU:0, one launch (start us, length us, event | category | flops | bytes accessed | tf_op | source)
XLA Modules:
  0.0 377.6 jit_solution(13928769380468582653)
XLA Ops:
  0.6 1.5 copy.53
  2.2 11.1 %all-to-all-start = ((s32[128,4,4]{2,1,0:T(4,128)}), s32[128,4,4]{2,1,0:T(4,128)S(1)}, u32[]{:S(2)}, u32[]{:S(2)}) async-start(s32[128,4,4]{2,1,0:T(4,128)} %bitcast.2), calls=%async_computation | async-start | bytes 524288 | tf_op jit(solution)/shard_map/all_to_all | solution.py:54
  13.3 1.1 reshape.82
  14.4 6.3 %convolution_convert_fusion.1 = bf16[128,4,8192]{2,0,1:T(8,128)(2,1)} fusion(bf16[16,8192,1]{1,0,2:T(8,128)(2,1)S(1)} %reshape.82, s32[128,4]{0,1:T(4,128)} %bitcast.67), kind=kOutput, calls=%fused_computation.17 | convolution fusion | flops 138420224 | bytes 8652800 | tf_op jit(solution)/shard_map/osq,qf->osf/dot_general | solution.py:46
  20.7 9.3 %copy.70 = bf16[64,8,64,128]{3,2,1,0:T(8,128)(2,1)} copy(bf16[64,8,64,128]{3,1,2,0:T(8,128)(2,1)} %bitcast.61) | data formatting | bytes 16777216
  30.0 9.6 %copy.55 = bf16[128,4,64,128]{3,2,1,0:T(8,128)(2,1)} copy(bf16[128,4,64,128]{3,2,0,1:T(8,128)(2,1)} %bitcast.62) | data formatting | bytes 16777216 | tf_op jit(solution)/shard_map/reshape | solution.py:49
  39.6 10.5 %all-to-all-start.1 = ((bf16[128,4,64,128]{3,2,1,0:T(8,128)(2,1)}), bf16[128,4,64,128]{3,2,1,0:T(8,128)(2,1)}, u32[]{:S(2)}, u32[]{:S(2)}) async-start(bf16[128,4,64,128]{3,2,1,0:T(8,128)(2,1)} %copy.55), calls=%async_computation.1 | async-start | bytes 16777216 | tf_op jit(solution)/shard_map/all_to_all | solution.py:53
  50.1 10.7 %copy.77 = bf16[16,8,192,128]{3,1,2,0:T(8,128)(2,1)} copy(bf16[16,8,192,128]{3,2,1,0:T(8,128)(2,1)} %bitcast.63) | data formatting | bytes 12582912
  60.9 0.1 copy.56
  61.0 88.6 %all-to-all-done.1 = bf16[128,4,64,128]{3,2,1,0:T(8,128)(2,1)} async-done(((bf16[128,4,64,128]{3,2,1,0:T(8,128)(2,1)}), bf16[128,4,64,128]{3,2,1,0:T(8,128)(2,1)}, u32[]{:S(2)}, u32[]{:S(2)}) %all-to-all-start.1) | async-done | bytes 8388640 | tf_op jit(solution)/shard_map/all_to_all | solution.py:53
  149.7 202.9 %while.11 = (s32[]{:T(128)}, f32[8,64,4]{1,0,2:T(8,128)S(1)}, s32[8,64,4]{1,2,0:T(4,128)S(1)}, s32[128]{0:T(128)S(1)}, bf16[128,24576]{1,0:T(8,128)(2,1)}, /*ind...) while((s32[]{:T(128)}, f32[8,64,4]{1,0,2:T(8,128)S(1)}, ...), condition=%wide.region_4.5_spmd.clone, body=%wide.region_0.4_spmd.clone.sunk | while | flops 2431778560 | bytes 57819240 | solution.py:35
  149.7 6.5 %convolution_convert_fusion.3 = bf16[64,4,24576]{2,0,1:T(8,128)(2,1)S(1)} fusion(bf16[128,24576]{1,0:T(8,128)(2,1)} %get-tuple-element.159, s32[64,4]{0,1:T(4,128)S(1)} %dynamic-slice_bitcast_fusion.2), kind=kOutput, calls=%fused_computation.1.clone.1 | convolution fusion | flops 1616936960 | bytes 18875392 | tf_op jit(solution)/shard_map/while/body/eval_jaxpr/gcn,nf->gcf/dot_general | solution.py:25
  156.2 6.8 %copy.84 = bf16[32,8,192,128]{3,2,1,0:T(8,128)(2,1)} copy(bf16[32,8,192,128]{3,1,2,0:T(8,128)(2,1)S(1)} %bitcast.58) | data formatting | bytes 25165824 | tf_op jit(solution)/shard_map/while
  162.9 0.2 fusion.26
  163.1 0.1 copy.83
  163.2 11.5 %fusion.27 = f32[64,4,64]{2,1,0:T(4,128)S(1)} fusion(s32[64,4]{1,0:T(8,128)S(1)} %copy.83, bf16[64,4,192,128]{3,2,0,1:T(8,128)(2,1)} %bitcast.59, bf16[8,64,64,128]{3,2,1,0:T(8,128)(2,1)} %get-tuple-element.160, s32[]{:T(128)} %get-tuple-element.146), kind=kOutput, calls=%fused_computation.3.clone.1 | convolution fusion | flops 814727168 | bytes 13698560 | tf_op jit(solution)/shard_map/while/body/eval_jaxpr/gqd,gcpd->gcqp/dot_general | solution.py:28
  174.7 0.1 reduce_sum.24
  175.0 6.5 %convolution_convert_fusion.3 = bf16[64,4,24576]{2,0,1:T(8,128)(2,1)S(1)} fusion(bf16[128,24576]{1,0:T(8,128)(2,1)} %get-tuple-element.159, s32[64,4]{0,1:T(4,128)S(1)} %dynamic-slice_bitcast_fusion.2), kind=kOutput, calls=%fused_computation.1.clone.1 | convolution fusion | flops 1616936960 | bytes 18875392 | tf_op jit(solution)/shard_map/while/body/eval_jaxpr/gcn,nf->gcf/dot_general | solution.py:25
  181.5 6.8 %copy.84 = bf16[32,8,192,128]{3,2,1,0:T(8,128)(2,1)} copy(bf16[32,8,192,128]{3,1,2,0:T(8,128)(2,1)S(1)} %bitcast.58) | data formatting | bytes 25165824 | tf_op jit(solution)/shard_map/while
  188.3 0.2 fusion.26
  188.6 11.5 %fusion.27 = f32[64,4,64]{2,1,0:T(4,128)S(1)} fusion(s32[64,4]{1,0:T(8,128)S(1)} %copy.83, bf16[64,4,192,128]{3,2,0,1:T(8,128)(2,1)} %bitcast.59, bf16[8,64,64,128]{3,2,1,0:T(8,128)(2,1)} %get-tuple-element.160, s32[]{:T(128)} %get-tuple-element.146), kind=kOutput, calls=%fused_computation.3.clone.1 | convolution fusion | flops 814727168 | bytes 13698560 | tf_op jit(solution)/shard_map/while/body/eval_jaxpr/gqd,gcpd->gcqp/dot_general | solution.py:28
  200.1 0.1 reduce_sum.24
  200.4 6.5 %convolution_convert_fusion.3 = bf16[64,4,24576]{2,0,1:T(8,128)(2,1)S(1)} fusion(bf16[128,24576]{1,0:T(8,128)(2,1)} %get-tuple-element.159, s32[64,4]{0,1:T(4,128)S(1)} %dynamic-slice_bitcast_fusion.2), kind=kOutput, calls=%fused_computation.1.clone.1 | convolution fusion | flops 1616936960 | bytes 18875392 | tf_op jit(solution)/shard_map/while/body/eval_jaxpr/gcn,nf->gcf/dot_general | solution.py:25
  206.9 6.8 %copy.84 = bf16[32,8,192,128]{3,2,1,0:T(8,128)(2,1)} copy(bf16[32,8,192,128]{3,1,2,0:T(8,128)(2,1)S(1)} %bitcast.58) | data formatting | bytes 25165824 | tf_op jit(solution)/shard_map/while
  213.7 0.2 fusion.26
  214.0 11.5 %fusion.27 = f32[64,4,64]{2,1,0:T(4,128)S(1)} fusion(s32[64,4]{1,0:T(8,128)S(1)} %copy.83, bf16[64,4,192,128]{3,2,0,1:T(8,128)(2,1)} %bitcast.59, bf16[8,64,64,128]{3,2,1,0:T(8,128)(2,1)} %get-tuple-element.160, s32[]{:T(128)} %get-tuple-element.146), kind=kOutput, calls=%fused_computation.3.clone.1 | convolution fusion | flops 814727168 | bytes 13698560 | tf_op jit(solution)/shard_map/while/body/eval_jaxpr/gqd,gcpd->gcqp/dot_general | solution.py:28
  225.5 0.1 reduce_sum.24
  225.8 6.5 %convolution_convert_fusion.3 = bf16[64,4,24576]{2,0,1:T(8,128)(2,1)S(1)} fusion(bf16[128,24576]{1,0:T(8,128)(2,1)} %get-tuple-element.159, s32[64,4]{0,1:T(4,128)S(1)} %dynamic-slice_bitcast_fusion.2), kind=kOutput, calls=%fused_computation.1.clone.1 | convolution fusion | flops 1616936960 | bytes 18875392 | tf_op jit(solution)/shard_map/while/body/eval_jaxpr/gcn,nf->gcf/dot_general | solution.py:25
  232.3 6.8 %copy.84 = bf16[32,8,192,128]{3,2,1,0:T(8,128)(2,1)} copy(bf16[32,8,192,128]{3,1,2,0:T(8,128)(2,1)S(1)} %bitcast.58) | data formatting | bytes 25165824 | tf_op jit(solution)/shard_map/while
  239.0 0.2 fusion.26
  239.4 11.5 %fusion.27 = f32[64,4,64]{2,1,0:T(4,128)S(1)} fusion(s32[64,4]{1,0:T(8,128)S(1)} %copy.83, bf16[64,4,192,128]{3,2,0,1:T(8,128)(2,1)} %bitcast.59, bf16[8,64,64,128]{3,2,1,0:T(8,128)(2,1)} %get-tuple-element.160, s32[]{:T(128)} %get-tuple-element.146), kind=kOutput, calls=%fused_computation.3.clone.1 | convolution fusion | flops 814727168 | bytes 13698560 | tf_op jit(solution)/shard_map/while/body/eval_jaxpr/gqd,gcpd->gcqp/dot_general | solution.py:28
  250.8 0.1 reduce_sum.24
  251.1 6.5 %convolution_convert_fusion.3 = bf16[64,4,24576]{2,0,1:T(8,128)(2,1)S(1)} fusion(bf16[128,24576]{1,0:T(8,128)(2,1)} %get-tuple-element.159, s32[64,4]{0,1:T(4,128)S(1)} %dynamic-slice_bitcast_fusion.2), kind=kOutput, calls=%fused_computation.1.clone.1 | convolution fusion | flops 1616936960 | bytes 18875392 | tf_op jit(solution)/shard_map/while/body/eval_jaxpr/gcn,nf->gcf/dot_general | solution.py:25
  257.6 6.8 %copy.84 = bf16[32,8,192,128]{3,2,1,0:T(8,128)(2,1)} copy(bf16[32,8,192,128]{3,1,2,0:T(8,128)(2,1)S(1)} %bitcast.58) | data formatting | bytes 25165824 | tf_op jit(solution)/shard_map/while
  264.4 0.2 fusion.26
  264.7 11.5 %fusion.27 = f32[64,4,64]{2,1,0:T(4,128)S(1)} fusion(s32[64,4]{1,0:T(8,128)S(1)} %copy.83, bf16[64,4,192,128]{3,2,0,1:T(8,128)(2,1)} %bitcast.59, bf16[8,64,64,128]{3,2,1,0:T(8,128)(2,1)} %get-tuple-element.160, s32[]{:T(128)} %get-tuple-element.146), kind=kOutput, calls=%fused_computation.3.clone.1 | convolution fusion | flops 814727168 | bytes 13698560 | tf_op jit(solution)/shard_map/while/body/eval_jaxpr/gqd,gcpd->gcqp/dot_general | solution.py:28
  276.2 0.1 reduce_sum.24
  276.5 6.5 %convolution_convert_fusion.3 = bf16[64,4,24576]{2,0,1:T(8,128)(2,1)S(1)} fusion(bf16[128,24576]{1,0:T(8,128)(2,1)} %get-tuple-element.159, s32[64,4]{0,1:T(4,128)S(1)} %dynamic-slice_bitcast_fusion.2), kind=kOutput, calls=%fused_computation.1.clone.1 | convolution fusion | flops 1616936960 | bytes 18875392 | tf_op jit(solution)/shard_map/while/body/eval_jaxpr/gcn,nf->gcf/dot_general | solution.py:25
  283.0 6.8 %copy.84 = bf16[32,8,192,128]{3,2,1,0:T(8,128)(2,1)} copy(bf16[32,8,192,128]{3,1,2,0:T(8,128)(2,1)S(1)} %bitcast.58) | data formatting | bytes 25165824 | tf_op jit(solution)/shard_map/while
  289.8 0.2 fusion.26
  290.1 11.5 %fusion.27 = f32[64,4,64]{2,1,0:T(4,128)S(1)} fusion(s32[64,4]{1,0:T(8,128)S(1)} %copy.83, bf16[64,4,192,128]{3,2,0,1:T(8,128)(2,1)} %bitcast.59, bf16[8,64,64,128]{3,2,1,0:T(8,128)(2,1)} %get-tuple-element.160, s32[]{:T(128)} %get-tuple-element.146), kind=kOutput, calls=%fused_computation.3.clone.1 | convolution fusion | flops 814727168 | bytes 13698560 | tf_op jit(solution)/shard_map/while/body/eval_jaxpr/gqd,gcpd->gcqp/dot_general | solution.py:28
  301.6 0.1 reduce_sum.24
  301.9 6.5 %convolution_convert_fusion.3 = bf16[64,4,24576]{2,0,1:T(8,128)(2,1)S(1)} fusion(bf16[128,24576]{1,0:T(8,128)(2,1)} %get-tuple-element.159, s32[64,4]{0,1:T(4,128)S(1)} %dynamic-slice_bitcast_fusion.2), kind=kOutput, calls=%fused_computation.1.clone.1 | convolution fusion | flops 1616936960 | bytes 18875392 | tf_op jit(solution)/shard_map/while/body/eval_jaxpr/gcn,nf->gcf/dot_general | solution.py:25
  308.4 6.8 %copy.84 = bf16[32,8,192,128]{3,2,1,0:T(8,128)(2,1)} copy(bf16[32,8,192,128]{3,1,2,0:T(8,128)(2,1)S(1)} %bitcast.58) | data formatting | bytes 25165824 | tf_op jit(solution)/shard_map/while
  315.1 0.2 fusion.26
  315.5 11.5 %fusion.27 = f32[64,4,64]{2,1,0:T(4,128)S(1)} fusion(s32[64,4]{1,0:T(8,128)S(1)} %copy.83, bf16[64,4,192,128]{3,2,0,1:T(8,128)(2,1)} %bitcast.59, bf16[8,64,64,128]{3,2,1,0:T(8,128)(2,1)} %get-tuple-element.160, s32[]{:T(128)} %get-tuple-element.146), kind=kOutput, calls=%fused_computation.3.clone.1 | convolution fusion | flops 814727168 | bytes 13698560 | tf_op jit(solution)/shard_map/while/body/eval_jaxpr/gqd,gcpd->gcqp/dot_general | solution.py:28
  327.0 0.1 reduce_sum.24
  327.3 6.5 %convolution_convert_fusion.3 = bf16[64,4,24576]{2,0,1:T(8,128)(2,1)S(1)} fusion(bf16[128,24576]{1,0:T(8,128)(2,1)} %get-tuple-element.159, s32[64,4]{0,1:T(4,128)S(1)} %dynamic-slice_bitcast_fusion.2), kind=kOutput, calls=%fused_computation.1.clone.1 | convolution fusion | flops 1616936960 | bytes 18875392 | tf_op jit(solution)/shard_map/while/body/eval_jaxpr/gcn,nf->gcf/dot_general | solution.py:25
  333.8 6.8 %copy.84 = bf16[32,8,192,128]{3,2,1,0:T(8,128)(2,1)} copy(bf16[32,8,192,128]{3,1,2,0:T(8,128)(2,1)S(1)} %bitcast.58) | data formatting | bytes 25165824 | tf_op jit(solution)/shard_map/while
  340.5 0.2 fusion.26
  340.7 0.1 copy.83
  340.8 11.5 %fusion.27 = f32[64,4,64]{2,1,0:T(4,128)S(1)} fusion(s32[64,4]{1,0:T(8,128)S(1)} %copy.83, bf16[64,4,192,128]{3,2,0,1:T(8,128)(2,1)} %bitcast.59, bf16[8,64,64,128]{3,2,1,0:T(8,128)(2,1)} %get-tuple-element.160, s32[]{:T(128)} %get-tuple-element.146), kind=kOutput, calls=%fused_computation.3.clone.1 | convolution fusion | flops 814727168 | bytes 13698560 | tf_op jit(solution)/shard_map/while/body/eval_jaxpr/gqd,gcpd->gcqp/dot_general | solution.py:28
  352.3 0.1 reduce_sum.24
  352.6 0.2 reshape.78
  352.8 0.9 copy.58
  353.6 11.1 %all-to-all-start.2 = ((f32[128,4,4]{1,2,0:T(4,128)}), f32[128,4,4]{1,2,0:T(4,128)S(1)}, u32[]{:S(2)}, u32[]{:S(2)}) async-start(f32[128,4,4]{1,2,0:T(4,128)} %copy.58), calls=%async_computation.2 | async-start | bytes 524288 | tf_op jit(solution)/shard_map/all_to_all | solution.py:56
  364.8 0.1 copy.52
  364.9 10.8 %all-to-all-done.2 = f32[128,4,4]{1,2,0:T(4,128)S(1)} async-done(((f32[128,4,4]{1,2,0:T(4,128)}), f32[128,4,4]{1,2,0:T(4,128)S(1)}, u32[]{:S(2)}, u32[]{:S(2)}) %all-to-all-start.2) | async-done | bytes 8224 | tf_op jit(solution)/shard_map/all_to_all | solution.py:56
  375.7 0.2 broadcast_select_fusion
  376.0 0.1 copy.59
  376.1 0.2 and_reduce_fusion
  376.3 0.1 fusion.15
  376.4 0.7 copy.61
  377.1 0.5 broadcast_select_fusion.1
  (51 shorter events, 1.7 us)
Async XLA Ops:
  2.2 37.4 %all-to-all-start = ((s32[128,4,4]{2,1,0:T(4,128)}), s32[128,4,4]{2,1,0:T(4,128)S(1)}, u32[]{:S(2)}, u32[]{:S(2)}) async-start(s32[128,4,4]{2,1,0:T(4,128)} %bitcast.2), calls=%async_computation | async-start | bytes 524288 | tf_op jit(solution)/shard_map/all_to_all | solution.py:54
  39.6 21.2 %copy-start.3 = (s32[1,128]{1,0:T(1,128)S(1)}, s32[1,128]{1,0:T(1,128)}, u32[]{:S(2)}) copy-start(s32[1,128]{1,0:T(1,128)} %param.13) | copy-start | bytes 1540
  39.6 110.0 %copy-start = (s32[128]{0:T(128)S(1)}, s32[128]{0:T(128)}, u32[]{:S(2)}) copy-start(s32[128]{0:T(128)} %param.11) | copy-start | bytes 1540
  39.6 110.0 %all-to-all-start.1 = ((bf16[128,4,64,128]{3,2,1,0:T(8,128)(2,1)}), bf16[128,4,64,128]{3,2,1,0:T(8,128)(2,1)}, u32[]{:S(2)}, u32[]{:S(2)}) async-start(bf16[128,4,64,128]{3,2,1,0:T(8,128)(2,1)} %copy.55), calls=%async_computation.1 | async-start | bytes 16777216 | tf_op jit(solution)/shard_map/all_to_all | solution.py:53
  149.6 215.1 %copy-start.1 = (s32[1,128,4]{1,2,0:T(4,128)S(1)}, s32[1,128,4]{1,2,0:T(4,128)}, u32[]{:S(2)}) copy-start(s32[1,128,4]{1,2,0:T(4,128)} %param.12) | copy-start | bytes 6148
  149.7 215.1 %copy-start.2 = (s32[1,128,4]{1,2,0:T(4,128)S(1)}, s32[1,128,4]{1,2,0:T(4,128)}, u32[]{:S(2)}) copy-start(s32[1,128,4]{1,2,0:T(4,128)} %param.15) | copy-start | bytes 6148
  353.6 22.1 %all-to-all-start.2 = ((f32[128,4,4]{1,2,0:T(4,128)}), f32[128,4,4]{1,2,0:T(4,128)S(1)}, u32[]{:S(2)}, u32[]{:S(2)}) async-start(f32[128,4,4]{1,2,0:T(4,128)} %copy.58), calls=%async_computation.2 | async-start | bytes 524288 | tf_op jit(solution)/shard_map/all_to_all | solution.py:56
where the time goes:
time: 379 us; the launch traced here: 378 us
  matrix products  150 us (40%)
  waiting for transfers between devices  99.4 us (26%)
  local copies, waits for them, and re-layouts  90.2 us (24%)
  starting transfers between devices  32.7 us (9%)
  other arithmetic  4 us (1%)
    dot_general x8, matrix products, one_block(): jnp.einsum('gqd,gcpd->gcqp', query_rows, passage_rows, preferred_element_...  91.9 us
    all_to_all x1, waiting for transfers between devices, body(): lax.all_to_all(outgoing, ('row', 'col'), split_axis=0, concat_axis=0, til...  88.6 us
    while x16, local copies, waits for them, and re-layouts  54.6 us
    dot_general x8, matrix products, one_block(): jnp.einsum('gcn,nf->gcf', selector, flat_pass, preferred_element_type=jnp...  52 us
    unnamed x13, local copies, waits for them, and re-layouts  22.4 us
    all_to_all x1, starting transfers between devices, body(): lax.all_to_all(cand_ids, ('row', 'col'), split_axis=0, concat_axis=0, til...  11.1 us
    all_to_all x1, starting transfers between devices, body(): lax.all_to_all(handled, ('row', 'col'), split_axis=0, concat_axis=0, tile...  11.1 us
    all_to_all x1, waiting for transfers between devices, body(): lax.all_to_all(handled, ('row', 'col'), split_axis=0, concat_axis=0, tile...  10.8 us
  transfers between devices with their start and end apart: 3, of which 2 were waited for; matrix products, arithmetic and copies ran while one was open for 10% of the time, Pallas kernels for 0%

commit v1 on v0

v1 whole, which is shorter than its diff:
```python
import jax
import jax.numpy as jnp
from jax import lax
from jax.experimental import pallas as pl
from jax.experimental.pallas import tpu as pltpu
from jax.sharding import PartitionSpec as P

LANE = 4
UNROLL = 4
MIB = 1 << 20


def smem():
    return pl.BlockSpec(memory_space=pltpu.SMEM)


def vmem():
    return pl.BlockSpec(memory_space=pltpu.VMEM)


def select_kernel(pick, table, out):
    slots = out.shape[0]

    def step(i, carry):
        for k in range(4):
            slot = i * 4 + k
            out[slot] = table[pick[slot]]
        return carry

    lax.fori_loop(0, slots // 4, step, 0)


def select(pick, table):
    shape = (pick.shape[0],) + table.shape[1:]
    return pl.pallas_call(
        select_kernel,
        out_shape=jax.ShapeDtypeStruct(shape, table.dtype),
        in_specs=[smem(), vmem()],
        out_specs=vmem(),
        compiler_params=pltpu.CompilerParams(vmem_limit_bytes=24 * MIB),
    )(pick, table)


def group_kernel(used, cand, group_pass, group_pair, count, filled, latest):
    pairs = cand.shape[0]
    caps = pairs // used.shape[0]

    def clear(i, carry):
        group_pass[i] = 0
        for k in range(LANE):
            group_pair[i * LANE + k] = pairs
        return carry

    lax.fori_loop(0, group_pass.shape[0], clear, 0)

    def clear_passage(i, carry):
        filled[i] = 0
        latest[i] = 0
        return carry

    lax.fori_loop(0, filled.shape[0], clear_passage, 0)

    def slot_step(slot, groups):
        def pair_step(k, groups):
            pair = slot * caps + k
            passage = cand[pair]
            have = filled[passage]
            place = have & (LANE - 1)
            fresh = (place == 0).astype(jnp.int32)
            group = jnp.where(place == 0, groups, latest[passage])
            latest[passage] = group
            filled[passage] = have + 1
            group_pass[group] = passage
            group_pair[group * LANE + place] = pair
            return groups + fresh

        return lax.fori_loop(0, used[slot], pair_step, groups)

    count[0] = lax.fori_loop(0, used.shape[0], slot_step, jnp.int32(0))


def group_pairs(used, cand, passages):
    most = (cand.shape[0] + (LANE - 1) * passages) // LANE
    most = -(-most // UNROLL) * UNROLL
    return pl.pallas_call(
        group_kernel,
        out_shape=(
            jax.ShapeDtypeStruct((most,), jnp.int32),
            jax.ShapeDtypeStruct((most * LANE,), jnp.int32),
            jax.ShapeDtypeStruct((1,), jnp.int32),
        ),
        in_specs=[smem(), smem()],
        out_specs=(smem(), smem(), smem()),
        scratch_shapes=[
            pltpu.SMEM((passages,), jnp.int32),
            pltpu.SMEM((passages,), jnp.int32),
        ],
    )(used, cand)


def score_kernel(group_pass, group_pair, count, rows, passages, out, peaks):
    slots, tokens, width = rows.shape
    pairs = out.shape[1]
    caps = pairs // slots
    peaks[...] = jnp.zeros_like(peaks)
    lower = lax.broadcasted_iota(jnp.int32, (1, 2 * tokens), 1) < tokens

    def step(i, carry):
        for u in range(UNROLL):
            group = i * UNROLL + u
            pair = [group_pair[group * LANE + k] for k in range(LANE)]
            picked = [rows[jnp.minimum(p // caps, slots - 1)] for p in pair]
            similar = lax.dot_general(
                passages[group_pass[group]],
                jnp.concatenate(picked, axis=0),
                (((1,), (1,)), ((), ())),
                preferred_element_type=jnp.float32,
            )
            top = jnp.max(similar, axis=0, keepdims=True)
            for k in range(0, LANE, 2):
                both = top[:, k * tokens : (k + 2) * tokens]
                peaks[pl.ds(pair[k], 1), :] = jnp.where(lower, both, 0.0)
                peaks[pl.ds(pair[k + 1], 1), :] = jnp.where(lower, 0.0, both)
        return carry

    steps = (count[0] + UNROLL - 1) // UNROLL
    lax.fori_loop(0, steps, step, 0)
    total = lax.dot_general(
        jnp.ones((8, 2 * tokens), jnp.float32),
        peaks[0:pairs, :],
        (((1,), (1,)), ((), ())),
        precision=lax.Precision.HIGHEST,
        preferred_element_type=jnp.float32,
    )
    out[...] = total[0:1] * (1.0 / tokens)


def score(groups, rows, passages):
    slots, tokens, width = rows.shape
    pairs = slots * 4
    return pl.pallas_call(
        score_kernel,
        out_shape=jax.ShapeDtypeStruct((1, pairs), jnp.float32),
        in_specs=[smem(), smem(), smem(), vmem(), vmem()],
        out_specs=vmem(),
        scratch_shapes=[pltpu.VMEM((pairs + 8, 2 * tokens), jnp.float32)],
        compiler_params=pltpu.CompilerParams(vmem_limit_bytes=40 * MIB),
    )(*groups, rows, passages)


def body(queries, passages, pass_len, send_cont, send_count, cand, cand_count):
    slot_list = send_cont[0]
    devices, slots = slot_list.shape
    caps = cand.shape[3]
    axes = ("row", "col")

    used = jnp.where(jnp.arange(slots)[None, :] < send_count[0][:, None], cand_count[0], 0)
    notes = jnp.concatenate([used, cand[0].reshape(devices, slots * caps)], axis=1)
    notes = lax.all_to_all(notes, axes, split_axis=0, concat_axis=0, tiled=True)
    outgoing = select(slot_list.reshape(-1), queries)
    outgoing = outgoing.reshape((devices, slots) + queries.shape[1:])
    rows = lax.all_to_all(outgoing, axes, split_axis=0, concat_axis=0, tiled=True)
    rows = rows.reshape((devices * slots,) + queries.shape[1:])

    tokens = lax.broadcasted_iota(jnp.int32, passages.shape[:2], 1)
    inside = tokens < pass_len[:, None]
    filled = jnp.where(inside[:, :, None], passages, passages[:, :1, :])
    groups = group_pairs(
        notes[:, :slots].reshape(-1), notes[:, slots:].reshape(-1), passages.shape[0]
    )
    handled = score(groups, rows, filled).reshape(devices, slots, caps)
    returned = lax.all_to_all(handled, axes, split_axis=0, concat_axis=0, tiled=True)

    live = jnp.arange(caps)[None, None, :] < used[:, :, None]
    scores = jnp.where(live, returned, 0.0)
    conts = jnp.arange(queries.shape[0])
    usable = live[:, :, :, None] & (slot_list[:, :, None] == conts)[:, :, None, :]
    best = jnp.max(jnp.where(usable, scores[:, :, :, None], -jnp.inf), axis=(0, 1, 2))
    best = jnp.where(jnp.any(usable, axis=(0, 1, 2)), best, 0.0)
    return scores[None], best


def solution(mesh):
    both = ("row", "col")
    in_specs = (
        P(both, None, None),
        P(both, None, None),
        P(both),
        P(both, None, None),
        P(both, None),
        P(both, None, None, None),
        P(both, None, None),
    )
    out_specs = (P(both, None, None, None), P(both))
    return jax.shard_map(body, mesh=mesh, in_specs=in_specs, out_specs=out_specs, check_vma=False)
```

time: 379 us -> 194 us (0.51)
  matrix products: 150 us -> 0 us
  local copies, waits for them, and re-layouts: 90.2 us -> 15 us
  Pallas kernels: 0 us -> 66.6 us
  waiting for transfers between devices: 99.4 us -> 72.7 us
  other arithmetic: 4 us -> 10 us
    dot_general x17 -> x0, matrix products: 150 us -> none  [the longest x8 91.9 us: one_block(): jnp.einsum('gqd,gcpd->gcqp', query_rows, passage_rows, preferred_element_...]
    pallas_call x0 -> x3, Pallas kernels: none -> 66.6 us  [the longest x1 33.4 us: score(): pl.pallas_call(score_kernel, out_shape=jax.ShapeDtypeStruct((1, pairs), j...]
    while x16 -> x0, local copies, waits for them, and re-layouts: 54.6 us -> none
    all_to_all x3, waiting for transfers between devices: 99.4 us -> 72.7 us  [the longest x1 59.2 us: body(): lax.all_to_all(outgoing, axes, split_axis=0, concat_axis=0, tiled=True)]
    unnamed x13 -> x17, local copies, waits for them, and re-layouts: 22.4 us -> 9.85 us
    reshape x4 -> x3, local copies, waits for them, and re-layouts: 11.7 us -> 2.45 us  [the longest x1 1.06 us: body(): handled = score(groups, rows, filled).reshape(devices, slots, caps)]
    select_n x2 -> x4, other arithmetic: 0.67 us -> 7.84 us  [the longest x1 6.44 us: body(): filled = jnp.where(inside[:, :, None], passages, passages[:, :1, :])]
  transfers between devices with their start and end apart: 3 -> 3, of which waited for: 2 -> 3; matrix products, arithmetic and copies ran while one was open for 10% -> 5% of each run, Pallas kernels for 0% -> 17%
where the time goes in v1:
time: 194 us
  waiting for transfers between devices  72.7 us (37%)
  Pallas kernels  66.6 us (34%)
  starting transfers between devices  29.2 us (15%)
  local copies, waits for them, and re-layouts  15 us (8%)
  other arithmetic  10 us (5%)
    all_to_all x1, waiting for transfers between devices, body(): lax.all_to_all(outgoing, axes, split_axis=0, concat_axis=0, tiled=True)  59.2 us
    pallas_call x1, Pallas kernels, score(): pl.pallas_call(score_kernel, out_shape=jax.ShapeDtypeStruct((1, pairs), j...  33.4 us
    pallas_call x1, Pallas kernels, group_pairs(): pl.pallas_call(group_kernel, out_shape=(jax.ShapeDtypeStruct((most,), jnp...  31.4 us
    all_to_all x1, starting transfers between devices, body(): notes = lax.all_to_all(notes, axes, split_axis=0, concat_axis=0, tiled=True)  11.1 us
    all_to_all x1, waiting for transfers between devices, body(): lax.all_to_all(handled, axes, split_axis=0, concat_axis=0, tiled=True)  10.8 us
    all_to_all x1, starting transfers between devices, body(): lax.all_to_all(handled, axes, split_axis=0, concat_axis=0, tiled=True)  10.4 us
    unnamed x17, local copies, waits for them, and re-layouts  9.85 us
    all_to_all x1, starting transfers between devices, body(): lax.all_to_all(outgoing, axes, split_axis=0, concat_axis=0, tiled=True)  7.63 us
  transfers between devices with their start and end apart: 3, of which 3 were waited for; matrix products, arithmetic and copies ran while one was open for 5% of the time, Pallas kernels for 17%

profile of v1, /device:TPU:0, one launch (start us, length us, event | category | flops | bytes accessed | tf_op | source)
XLA Modules:
  0.0 194.2 jit_solution(11538916867798390603)
XLA Ops:
  0.6 0.7 bitcast_select_fusion
  1.3 0.7 pad_add_fusion
  2.0 0.7 copy.27
  2.7 11.1 %all-to-all-start = ((s32[128,1,20]{2,1,0:T(1,128)}), s32[128,1,20]{2,1,0:T(1,128)S(1)}, u32[]{:S(2)}, u32[]{:S(2)}) async-start(s32[128,1,20]{2,1,0:T(1,128)} %bitcast.3), calls=%async_computation | async-start | bytes 131072 | tf_op jit(solution)/shard_map/all_to_all | solution.py:159
  13.9 0.8 copy.28
  14.7 0.1 reshape_squeeze.7.pick
  14.8 0.0 copy-start.2
  14.8 0.9 copy-done.2
  15.7 1.8 shard_map.87
  17.5 0.0 copy-start
  17.5 3.2 %copy-done = bf16[512,64,128]{2,1,0:T(8,128)(2,1)} copy-done((bf16[512,64,128]{2,1,0:T(8,128)(2,1)}, bf16[512,64,128]{2,1,0:T(8,128)(2,1)S(1)}, u32[]{:S(2)}) %copy-start) | copy-done | bytes 8388632
  20.7 2.7 %all-to-all-done = s32[128,1,20]{2,1,0:T(1,128)S(1)} async-done(((s32[128,1,20]{2,1,0:T(1,128)}), s32[128,1,20]{2,1,0:T(1,128)S(1)}, u32[]{:S(2)}, u32[]{:S(2)}) %all-to-all-start) | async-done | bytes 10272 | tf_op jit(solution)/shard_map/all_to_all | solution.py:159
  23.4 0.0 copy-start.5
  23.4 0.0 copy-start.6
  23.4 7.6 %all-to-all-start.1 = ((bf16[128,4,64,128]{3,2,1,0:T(8,128)(2,1)}), bf16[128,4,64,128]{3,2,1,0:T(8,128)(2,1)}, u32[]{:S(2)}, u32[]{:S(2)}) async-start(bf16[128,4,64,128]{3,2,1,0:T(8,128)(2,1)} %bitcast.15), calls=%async_computation.1 | async-start | bytes 16777216 | tf_op jit(solution)/shard_map/all_to_all | solution.py:162
  31.1 0.1 copy.26
  31.2 1.0 slice.11
  32.2 0.2 iota_compare_fusion
  32.4 0.1 copy.30
  32.5 0.0 copy-done.5
  32.5 0.0 copy-done.6
  32.6 0.1 iota_compare_fusion.1
  32.7 6.4 %broadcast_select_fusion.passages = bf16[128,192,128]{2,1,0:T(8,128)(2,1)} fusion(bf16[128,192,128]{2,1,0:T(8,128)(2,1)} %param.8, pred[128,192]{1,0:T(8,128)(4,1)S(1)} %iota_compare_fusion.1, bf16[128,128]{1,0:T(8,128)(2,1)S(1)} %bitcast.18), kind=kLoop, calls=%fused_computation | loop fusion | flops 3145728 | bytes 12640256 | tf_op jit(solution)/shard_map/jit(_where)/select_n | solution.py:167
  39.1 0.1 slice.13
  39.2 0.7 reshape.78.cand
  39.9 0.7 reshape.77.used
  40.6 31.4 %shard_map.86 = (s32[608]{0:T(1024)}, s32[2432]{0:T(1024)}, s32[1]{0:T(128)}) custom-call(s32[512]{0:T(512)} %reshape.77.used, s32[2048]{0:T(1024)} %reshape.78.cand), custom_call_target="tpu_custom_call" | custom-call | tf_op jit(solution)/shard_map/pallas_call | solution.py:85
  72.0 59.2 %all-to-all-done.1 = bf16[128,4,64,128]{3,2,1,0:T(8,128)(2,1)} async-done(((bf16[128,4,64,128]{3,2,1,0:T(8,128)(2,1)}), bf16[128,4,64,128]{3,2,1,0:T(8,128)(2,1)}, u32[]{:S(2)}, u32[]{:S(2)}) %all-to-all-start.1) | async-done | bytes 8388640 | tf_op jit(solution)/shard_map/all_to_all | solution.py:162
  131.2 0.0 copy-start.1
  131.2 2.8 %copy-done.1 = bf16[128,192,128]{2,1,0:T(8,128)(2,1)S(1)} copy-done((bf16[128,192,128]{2,1,0:T(8,128)(2,1)S(1)}, bf16[128,192,128]{2,1,0:T(8,128)(2,1)}, u32[]{:S(2)}) %copy-start.1) | copy-done | bytes 6291480
  134.0 0.0 copy-start.3
  134.0 0.7 copy-done.3
  134.7 0.0 copy-start.4
  134.7 0.7 copy-done.4
  135.4 33.4 %shard_map.88 = f32[1,2048]{1,0:T(1,128)S(1)} custom-call(s32[608]{0:T(1024)S(1)} %copy-done.4, s32[2432]{0:T(1024)S(1)} %copy-done.3, s32[1]{0:T(128)} %get-tuple-element.7.count, bf16[512,64,128]{2,1,0:T(8,128)(2,1)} %bitcast.6.rows, bf16[128,192,128]{2,1,0:T(8,128)(2,1)S(1)} %copy-done.1), custom_call_target="tpu_custom_call" | custom-call | tf_op jit(solution)/shard_map/pallas_call | solution.py:141
  168.7 0.5 broadcast.43
  169.3 0.7 reduce.3
  169.9 1.1 reshape.81
  171.0 10.4 %all-to-all-start.2 = ((f32[128,4,4]{2,1,0:T(4,128)}), f32[128,4,4]{2,1,0:T(4,128)S(1)}, u32[]{:S(2)}, u32[]{:S(2)}) async-start(f32[128,4,4]{2,1,0:T(4,128)} %reshape.81), calls=%async_computation.2 | async-start | bytes 524288 | tf_op jit(solution)/shard_map/all_to_all | solution.py:172
  181.4 0.1 and_reduce_fusion
  181.5 10.8 %all-to-all-done.2 = f32[128,4,4]{2,1,0:T(4,128)S(1)} async-done(((f32[128,4,4]{2,1,0:T(4,128)}), f32[128,4,4]{2,1,0:T(4,128)S(1)}, u32[]{:S(2)}, u32[]{:S(2)}) %all-to-all-start.2) | async-done | bytes 8224 | tf_op jit(solution)/shard_map/all_to_all | solution.py:172
  192.3 0.2 broadcast_select_fusion.1
  192.5 0.1 copy.31
  192.6 0.2 fusion
  192.8 0.2 fusion.1
  193.0 0.7 copy.32
  193.7 0.5 broadcast_select_fusion.2
  (2 shorter events, 0.0 us)
Async XLA Ops:
  2.7 20.7 %all-to-all-start = ((s32[128,1,20]{2,1,0:T(1,128)}), s32[128,1,20]{2,1,0:T(1,128)S(1)}, u32[]{:S(2)}, u32[]{:S(2)}) async-start(s32[128,1,20]{2,1,0:T(1,128)} %bitcast.3), calls=%async_computation | async-start | bytes 131072 | tf_op jit(solution)/shard_map/all_to_all | solution.py:159
  14.8 1.0 copy-start.2
  17.5 3.2 %copy-start = (bf16[512,64,128]{2,1,0:T(8,128)(2,1)}, bf16[512,64,128]{2,1,0:T(8,128)(2,1)S(1)}, u32[]{:S(2)}) copy-start(bf16[512,64,128]{2,1,0:T(8,128)(2,1)S(1)} %shard_map.87) | copy-start | bytes 25165828
  23.4 9.1 %copy-start.5 = (s32[1,128,4]{1,2,0:T(4,128)S(1)}, s32[1,128,4]{1,2,0:T(4,128)}, u32[]{:S(2)}) copy-start(s32[1,128,4]{1,2,0:T(4,128)} %param.10) | copy-start | bytes 6148
  23.4 9.1 %copy-start.6 = (s32[128]{0:T(128)S(1)}, s32[128]{0:T(128)}, u32[]{:S(2)}) copy-start(s32[128]{0:T(128)} %param.9) | copy-start | bytes 1540
  23.4 107.8 %all-to-all-start.1 = ((bf16[128,4,64,128]{3,2,1,0:T(8,128)(2,1)}), bf16[128,4,64,128]{3,2,1,0:T(8,128)(2,1)}, u32[]{:S(2)}, u32[]{:S(2)}) async-start(bf16[128,4,64,128]{3,2,1,0:T(8,128)(2,1)} %bitcast.15), calls=%async_computation.1 | async-start | bytes 16777216 | tf_op jit(solution)/shard_map/all_to_all | solution.py:162
  131.2 2.8 %copy-start.1 = (bf16[128,192,128]{2,1,0:T(8,128)(2,1)S(1)}, bf16[128,192,128]{2,1,0:T(8,128)(2,1)}, u32[]{:S(2)}) copy-start(bf16[128,192,128]{2,1,0:T(8,128)(2,1)} %broadcast_select_fusion.passages) | copy-start | bytes 18874372
  134.0 0.7 copy-start.3
  134.7 0.7 copy-start.4
  171.0 21.3 %all-to-all-start.2 = ((f32[128,4,4]{2,1,0:T(4,128)}), f32[128,4,4]{2,1,0:T(4,128)S(1)}, u32[]{:S(2)}, u32[]{:S(2)}) async-start(f32[128,4,4]{2,1,0:T(4,128)} %reshape.81), calls=%async_computation.2 | async-start | bytes 524288 | tf_op jit(solution)/shard_map/all_to_all | solution.py:172

commit v2 on v0

v2 whole, which is shorter than its diff:
```python
import itertools

import jax
import jax.numpy as jnp
from jax import lax
from jax.experimental import pallas as pl
from jax.experimental.pallas import tpu as pltpu
from jax.sharding import Mesh, PartitionSpec as P

ALL = ("y", "x", "z", "core")
PLACE = ("y", "x", "z")
SIDE = 4
CHIPS = SIDE**3
EARLY = CHIPS * 3 // 4
CAPS = 4
SLOTS = 4
LANE = 4
UNROLL = 16
MIB = 1 << 20
CONTS = 16
NOTE_ROWS = 16
NOTES = 128

ORDERS = (("x", "y", "z"), ("y", "z", "x"))


def smem():
    return pl.BlockSpec(memory_space=pltpu.SMEM)


def vmem():
    return pl.BlockSpec(memory_space=pltpu.VMEM)


def hbm():
    return pl.BlockSpec(memory_space=pl.ANY)


def shift(array, stage, by):
    pairs = []
    for y, x, z, core in itertools.product(range(SIDE), range(SIDE), range(SIDE), range(2)):
        at = {"y": y, "x": x, "z": z}
        axis = ORDERS[core][stage]
        to = dict(at, **{axis: (at[axis] + by) % SIDE})
        pairs.append(tuple(((p["y"] * SIDE + p["x"]) * SIDE + p["z"]) * 2 + core for p in (at, to)))
    return lax.ppermute(array, ALL, pairs)


def cost(us):
    return pl.CostEstimate(flops=0, bytes_accessed=int(us * 3_500_000), transcendentals=0)


def chip_low(at, low):
    y, x, z = ((at[k] - low[k]) & (SIDE - 1) for k in "yxz")
    return (y * SIDE + x) * SIDE + z


def by_core(core, digits):
    low = [dict(zip(order, digits)) for order in ORDERS]
    return {k: jnp.where(core == 0, low[0][k], low[1][k]) for k in "yxz"}


def select_kernel(targets, here, after, *refs):
    planes, outs = refs[:SIDE], refs[SIDE : SIDE + len(targets)]
    table, notes, arrived = refs[SIDE + len(targets) :]
    at, core = dict(zip("yxz", (here[0], here[1], here[2]))), here[3]
    end = planes[0].shape[1] - NOTE_ROWS
    tokens = end // CONTS
    for source in range(SIDE * SIDE):
        told = planes[source // SIDE][source % SIDE, end : end + NOTE_ROWS, :]
        table[source] = told.astype(jnp.float32).astype(jnp.int32)[:8]
    copy = pltpu.make_async_copy(table, notes, arrived)
    copy.start()
    owners = []
    for third in targets:
        chip = chip_low(at, by_core(core, (0, 0, -third)))
        owners += [(chip * 2 + core) * SLOTS, (chip * 2 + 1 - core) * SLOTS]
    copy.wait()
    for second in range(SIDE):

        def step(first, carry):
            source = second * SIDE + first
            for out, target in enumerate(outs):
                for slot in range(2 * SLOTS):
                    start = owners[out * 2 + slot // SLOTS]
                    cont = notes[source, start >> 7, (start & 127) + slot % SLOTS]
                    rows = pl.ds(pl.multiple_of(cont * tokens, 16), tokens)
                    target[source * 2 * SLOTS + slot] = planes[second][first, rows, :]
            return carry

        lax.fori_loop(0, SIDE, step, 0)


def select(targets, here, after, planes):
    tokens = (planes[0].shape[1] - NOTE_ROWS) // CONTS
    shape = (SIDE * SIDE * 2 * SLOTS, tokens, planes[0].shape[2])
    return pl.pallas_call(
        lambda *refs: select_kernel(targets, *refs),
        out_shape=[jax.ShapeDtypeStruct(shape, planes[0].dtype)] * len(targets),
        in_specs=[smem(), hbm()] + [vmem()] * SIDE,
        out_specs=[vmem()] * len(targets),
        cost_estimate=cost(4),
        scratch_shapes=[
            pltpu.VMEM((SIDE * SIDE, 8, 128), jnp.int32),
            pltpu.SMEM((SIDE * SIDE, 8, 128), jnp.int32),
            pltpu.SemaphoreType.DMA(()),
        ],
        compiler_params=pltpu.CompilerParams(vmem_limit_bytes=8 * MIB),
    )(here, after, *planes)


def group_kernel(here, notes, after, *refs):
    parts, states = refs[:2], refs[2:]
    nobody = CHIPS * 2 * SLOTS * CAPS
    size = parts[0].shape[0] // 2
    most = (size - 1) // (LANE + 1)
    passages = states[0].shape[0] - 8
    at, core = dict(zip("yxz", (here[0], here[1], here[2]))), here[3]

    def clear(i, carry):
        for u in range(4):
            for groups in parts:
                for start in (0, size):
                    groups[start + most * LANE + i * 4 + u] = 0
                    for k in range(LANE):
                        groups[start + (i * 4 + u) * LANE + k] = nobody
        return carry

    lax.fori_loop(0, most // 4, clear, 0)

    def clear_passage(i, carry):
        for u in range(4):
            for state in states:
                state[i * 4 + u] = 0
        return carry

    lax.fori_loop(0, states[0].shape[0] // 4, clear_passage, 0)

    def sources(first, last, part, ends):
        def source_step(source, ends):
            third = source // (SIDE * SIDE)
            third = third + (third == 2).astype(jnp.int32) - (third == 3).astype(jnp.int32)
            digits = (source % SIDE, source // SIDE % SIDE, third)
            chip = chip_low(at, by_core(core, digits))
            base = chip * NOTES
            ends = list(ends)
            row = chip * (2 * SLOTS * CAPS)
            code = ((source - first) * 2 * SLOTS << 12) | row
            for j in range(SLOTS):
                for which in range(2):
                    groups, state = parts[part], states[part * 2 + which]
                    info = base + which * SLOTS * (1 + CAPS)
                    used = notes[info + j]
                    for k in range(CAPS):
                        slot = which * SLOTS + j
                        passage = notes[info + SLOTS + j * CAPS + k]
                        live = k < used
                        at_state = jnp.where(live, passage, passages)
                        spot = state[at_state]
                        fresh = (spot & (LANE - 1)) == 0
                        spot = jnp.where(fresh, ends[which], spot)
                        state[at_state] = spot + 1
                        spot = jnp.where(live, spot, (most - 1) * LANE)
                        groups[which * size + most * LANE + (spot >> 2)] = passage
                        groups[which * size + spot] = code + ((slot << 12) | (slot * CAPS + k))
                        ends[which] = jnp.where(live & fresh, ends[which] + LANE, ends[which])
            return tuple(ends)

        return lax.fori_loop(first, last, source_step, ends)

    zero = jnp.int32(0)
    for part, (first, last) in enumerate(((0, EARLY), (EARLY, CHIPS))):
        ends = sources(first, last, part, (zero, zero))
        for which in range(2):
            parts[part][which * size + most * (LANE + 1)] = ends[which] // LANE


def group_pairs(here, notes, after, passages):
    most = (EARLY * SLOTS * CAPS + (LANE - 1) * passages) // LANE
    most = (most // UNROLL + 2) * UNROLL
    return pl.pallas_call(
        group_kernel,
        out_shape=[jax.ShapeDtypeStruct((2 * (most * (LANE + 1) + 1),), jnp.int32)] * 2,
        in_specs=[smem(), smem(), hbm()],
        out_specs=[smem()] * 2,
        scratch_shapes=[pltpu.SMEM((passages + 8,), jnp.int32)] * 4,
        cost_estimate=cost(10),
    )(here, notes, after)


def score_kernel(many, groups, lengths, *refs):
    pieces, refs = refs[:many], refs[many:]
    own, sibling, refs = refs[0], refs[1], refs[2:]
    if many > 1:
        out, rows, arrived, peaks = refs
        each = pieces[0].shape[0]
        copies = [
            pltpu.make_async_copy(piece, rows.at[pl.ds(i * each, each)], arrived.at[i])
            for i, piece in enumerate(pieces)
        ]
        for copy in copies:
            copy.start()
        peaks[...] = jnp.zeros_like(peaks)
        for copy in copies:
            copy.wait()
    else:
        before, out, peaks = refs
        rows = pieces[0]
        peaks[...] = jnp.zeros_like(peaks)

    size = groups.shape[0] // 2
    most = (size - 1) // (LANE + 1)
    tokens = rows.shape[1]
    pairs = peaks.shape[0] - 8
    lower = lax.broadcasted_iota(jnp.int32, (1, 2 * tokens), 1) < tokens
    token = lax.broadcasted_iota(jnp.int32, (own.shape[1], LANE * tokens), 0)
    for which, texts in enumerate((own, sibling)):
        start = which * size

        def step(i, carry):
            for u in range(UNROLL):
                group = i * UNROLL + u
                code = [groups[start + group * LANE + k] for k in range(LANE)]
                passage = groups[start + most * LANE + group]
                similar = lax.dot_general(
                    texts[passage],
                    jnp.concatenate([rows[c >> 12] for c in code], axis=0),
                    (((1,), (1,)), ((), ())),
                    preferred_element_type=jnp.float32,
                )
                inside = token < lengths[which * own.shape[0] + passage]
                top = jnp.max(jnp.where(inside, similar, -jnp.inf), axis=0, keepdims=True)
                for k in range(0, LANE, 2):
                    both = top[:, k * tokens : (k + 2) * tokens]
                    peaks[pl.ds(code[k] & 4095, 1), :] = jnp.where(lower, both, 0.0)
                    peaks[pl.ds(code[k + 1] & 4095, 1), :] = jnp.where(lower, 0.0, both)
            return carry

        steps = (groups[start + most * (LANE + 1)] + UNROLL - 1) // UNROLL
        lax.fori_loop(0, steps, step, 0)
    high = peaks[0:pairs, :].astype(jnp.bfloat16)
    low = (peaks[0:pairs, :] - high.astype(jnp.float32)).astype(jnp.bfloat16)
    ones = jnp.ones((16, 2 * tokens), jnp.bfloat16)
    total = sum(
        lax.dot_general(
            ones, part, (((1,), (1,)), ((), ())), preferred_element_type=jnp.float32
        )
        for part in (high, low)
    )
    total = total[0:1] * (1.0 / tokens)
    each = out.shape[1]
    for chip in range(CHIPS):
        out[chip : chip + 1, :] = total[:, chip * each : (chip + 1) * each]
    if many == 1:
        out[...] = out[...] + before[...]


def score(groups, lengths, pieces, own, sibling, before=()):
    pairs = CHIPS * 2 * SLOTS * CAPS
    many = len(pieces)
    tokens = pieces[0].shape[1]
    scratch = [pltpu.VMEM((pairs + 8, 2 * tokens), jnp.float32)]
    if many > 1:
        scratch = [
            pltpu.VMEM((many * pieces[0].shape[0],) + pieces[0].shape[1:], own.dtype),
            pltpu.SemaphoreType.DMA((many,)),
        ] + scratch
    return pl.pallas_call(
        lambda *refs: score_kernel(many, *refs),
        out_shape=jax.ShapeDtypeStruct((CHIPS, pairs // CHIPS), jnp.float32),
        in_specs=[smem()] * 2
        + [hbm() if many > 1 else vmem()] * many
        + [vmem()] * (2 + len(before)),
        out_specs=vmem(),
        scratch_shapes=scratch,
        cost_estimate=cost(12 if many > 1 else 8),
        compiler_params=pltpu.CompilerParams(vmem_limit_bytes=16 * MIB),
    )(groups, lengths, *pieces, own, sibling, *before)


def body(queries, passages, pass_len, send_cont, send_count, cand, cand_count):
    slot_list = send_cont[0]
    devices, slots = slot_list.shape
    caps = cand.shape[3]
    core = lax.axis_index("core")
    here = jnp.stack([lax.axis_index(k) for k in ALL]).astype(jnp.int32)

    used = jnp.where(jnp.arange(slots)[None, :] < send_count[0][:, None], cand_count[0], 0)
    info = jnp.concatenate([used, cand[0].reshape(devices, slots * caps)], axis=1)
    info = info.reshape(CHIPS, 2, -1)
    info = jnp.where(core == 0, info, info[:, ::-1]).reshape(CHIPS, -1)
    info = jnp.pad(info, ((0, 0), (0, NOTES - info.shape[1])))

    told = slot_list.astype(queries.dtype).reshape(-1, 128)
    told = jnp.pad(told, ((0, NOTE_ROWS - told.shape[0]), (0, 0)))
    piece = jnp.concatenate([queries.reshape(-1, queries.shape[2]), told], axis=0)
    line = jnp.stack([piece] + [shift(piece, 0, by) for by in range(1, SIDE)])
    planes = [line] + [shift(line, 1, by) for by in range(1, SIDE)]
    info, _ = lax.optimization_barrier((info, line))
    notes = lax.all_to_all(info, PLACE, split_axis=0, concat_axis=0, tiled=True)

    swap = [(0, 1), (1, 0)]
    sibling = lax.ppermute(passages, "core", swap)
    lengths = jnp.concatenate([pass_len, lax.ppermute(pass_len, "core", swap)])

    up, down = select((1, 3), here, notes, planes)
    near, back = shift(up, 2, 1), shift(down, 2, 3)
    across, here_rows = select((2, 0), here, up, planes)
    early, late = group_pairs(here, notes.reshape(-1), here_rows, passages.shape[0])
    across, early = lax.optimization_barrier((across, early))
    far = shift(across, 2, 2)
    handled = score(early, lengths, [here_rows, near, back], passages, sibling)
    handled = score(late, lengths, [far], passages, sibling, (handled,))
    returned = lax.all_to_all(handled, PLACE, split_axis=0, concat_axis=0, tiled=True)
    returned = returned.reshape(CHIPS, 2, -1)
    returned = jnp.where(core == 0, returned, returned[:, ::-1])
    returned = returned.reshape(devices, slots, caps)

    live = jnp.arange(caps)[None, None, :] < used[:, :, None]
    scores = jnp.where(live, returned, 0.0)
    conts = jnp.arange(queries.shape[0])
    usable = live[:, :, :, None] & (slot_list[:, :, None] == conts)[:, :, None, :]
    best = jnp.max(jnp.where(usable, scores[:, :, :, None], -jnp.inf), axis=(0, 1, 2))
    best = jnp.where(jnp.any(usable, axis=(0, 1, 2)), best, 0.0)
    return scores[None], best


def solution(mesh):
    mesh = Mesh(mesh.devices.reshape(SIDE, SIDE, SIDE, 2), ALL)
    in_specs = (
        P(ALL, None, None),
        P(ALL, None, None),
        P(ALL),
        P(ALL, None, None),
        P(ALL, None),
        P(ALL, None, None, None),
        P(ALL, None, None),
    )
    out_specs = (P(ALL, None, None, None), P(ALL))
    return jax.shard_map(body, mesh=mesh, in_specs=in_specs, out_specs=out_specs, check_vma=False)
```

time: 379 us -> 144 us (0.38)
  matrix products: 150 us -> 0 us
  local copies, waits for them, and re-layouts: 90.2 us -> 10.1 us
  waiting for transfers between devices: 99.4 us -> 42.7 us
  Pallas kernels: 0 us -> 52.2 us
    dot_general x17 -> x0, matrix products: 150 us -> none  [the longest x8 91.9 us: one_block(): jnp.einsum('gqd,gcpd->gcqp', query_rows, passage_rows, preferred_element_...]
    all_to_all x3 -> x2, waiting for transfers between devices: 99.4 us -> 25.3 us  [the longest x1 15.8 us: body(): notes = lax.all_to_all(info, PLACE, split_axis=0, concat_axis=0, tiled=True)]
    while x16 -> x0, local copies, waits for them, and re-layouts: 54.6 us -> none
    pallas_call x0 -> x5, Pallas kernels: none -> 52.2 us  [the longest x1 22.1 us: group_pairs(): pl.pallas_call(group_kernel, out_shape=[jax.ShapeDtypeStruct((2 * (most *...]
    ppermute x0 -> x11, waiting for transfers between devices: none -> 17.4 us  [the longest x9 16.8 us: shift(): return lax.ppermute(array, ALL, pairs)]
    ppermute x0 -> x11, starting transfers between devices: none -> 14.8 us  [the longest x9 14.8 us: shift(): return lax.ppermute(array, ALL, pairs)]
    unnamed x13 -> x33, local copies, waits for them, and re-layouts: 22.4 us -> 7.69 us
    all_to_all x3 -> x2, starting transfers between devices: 32.7 us -> 18.7 us  [the longest x1 10.8 us: body(): lax.all_to_all(handled, PLACE, split_axis=0, concat_axis=0, tiled=True)]
  transfers between devices with their start and end apart: 3 -> 13, of which waited for: 2 -> 7; matrix products, arithmetic and copies ran while one was open for 10% -> 4% of each run, Pallas kernels for 0% -> 31%
where the time goes in v2:
time: 144 us
  Pallas kernels  52.2 us (36%)
  waiting for transfers between devices  42.7 us (30%)
  starting transfers between devices  33.5 us (23%)
  local copies, waits for them, and re-layouts  10.1 us (7%)
  other arithmetic  4.22 us (3%)
    pallas_call x1, Pallas kernels, group_pairs(): pl.pallas_call(group_kernel, out_shape=[jax.ShapeDtypeStruct((2 * (most *...  22.1 us
    pallas_call x2, Pallas kernels, score(): pl.pallas_call(lambda *refs: score_kernel(many, *refs), out_shape=jax.Sha...  20.4 us
    ppermute x9, waiting for transfers between devices, shift(): return lax.ppermute(array, ALL, pairs)  16.8 us
    all_to_all x1, waiting for transfers between devices, body(): notes = lax.all_to_all(info, PLACE, split_axis=0, concat_axis=0, tiled=True)  15.8 us
    ppermute x9, starting transfers between devices, shift(): return lax.ppermute(array, ALL, pairs)  14.8 us
    all_to_all x1, starting transfers between devices, body(): lax.all_to_all(handled, PLACE, split_axis=0, concat_axis=0, tiled=True)  10.8 us
    pallas_call x2, Pallas kernels, select(): pl.pallas_call(lambda *refs: select_kernel(targets, *refs), out_shape=[ja...  9.67 us
    all_to_all x1, waiting for transfers between devices, body(): lax.all_to_all(handled, PLACE, split_axis=0, concat_axis=0, tiled=True)  9.41 us
  transfers between devices with their start and end apart: 13, of which 7 were waited for; matrix products, arithmetic and copies ran while one was open for 4% of the time, Pallas kernels for 31%

profile of v2, /device:TPU:0, one launch (start us, length us, event | category | flops | bytes accessed | tf_op | source)
XLA Modules:
  0.0 143.6 jit_solution(6623214936519080095)
XLA Ops:
  0.6 0.1 collective-permute-start.8
  0.7 0.7 convert_element_type.9
  1.4 0.1 copy.48
  1.6 0.1 convert_element_type.10
  1.7 1.0 fusion.4
  2.7 3.2 %collective-permute-start.1 = (bf16[1040,128]{1,0:T(8,128)(2,1)S(1)}, bf16[1040,128]{1,0:T(8,128)(2,1)S(1)}, u32[]{:S(2)}, u32[]{:S(2)}) collective-permute-start(bf16[1040,128]{1,0:T(8,128)(2,1)S(1)} %get-tuple-element.27), channel_id=1, source_target_pairs={{0,16},{1,65},{2,18},{3,67},{4,20},{5,69},{6,22},{7,71},{8,24},{9,... | collective-permute-start | bytes 798728 | tf_op jit(solution)/shard_map/ppermute | solution.py:46
  5.9 1.1 collective-permute-start.2
  7.0 0.9 collective-permute-start
  7.9 2.8 %collective-permute-done.1 = bf16[1040,128]{1,0:T(8,128)(2,1)S(1)} collective-permute-done((bf16[1040,128]{1,0:T(8,128)(2,1)S(1)}, bf16[1040,128]{1,0:T(8,128)(2,1)S(1)}, u32[]{:S(2)}, u32[]{:S(2)}) %collective-permute-start.1) | collective-permute-done | bytes 266272 | tf_op jit(solution)/shard_map/ppermute | solution.py:46
  10.7 3.0 %collective-permute-done.2 = bf16[1040,128]{1,0:T(8,128)(2,1)S(1)} collective-permute-done((bf16[1040,128]{1,0:T(8,128)(2,1)S(1)}, bf16[1040,128]{1,0:T(8,128)(2,1)S(1)}, u32[]{:S(2)}, u32[]{:S(2)}) %collective-permute-start.2) | collective-permute-done | bytes 266272 | tf_op jit(solution)/shard_map/ppermute | solution.py:46
  13.7 0.9 collective-permute-done
  14.7 0.1 pad_maximum_fusion.refs_2_
  14.8 1.6 %collective-permute-start.3 = (bf16[4,1040,128]{2,1,0:T(8,128)(2,1)S(1)}, bf16[4,1040,128]{2,1,0:T(8,128)(2,1)S(1)}, u32[]{:S(2)}, u32[]{:S(2)}) collective-permute-start(bf16[4,1040,128]{2,1,0:T(8,128)(2,1)S(1)} %pad_maximum_fusion.refs_2_), channel_id=1, source_target_pairs={{0,32},{1,3},{2,34},{3,5},{4,36},{5,7},{6,38},{7,1},{8,40},{9,11},... | collective-permute-start | bytes 3194888 | tf_op jit(solution)/shard_map/ppermute | solution.py:46
  16.4 2.9 %collective-permute-start.4 = (bf16[4,1040,128]{2,1,0:T(8,128)(2,1)S(1)}, bf16[4,1040,128]{2,1,0:T(8,128)(2,1)S(1)}, u32[]{:S(2)}, u32[]{:S(2)}) collective-permute-start(bf16[4,1040,128]{2,1,0:T(8,128)(2,1)S(1)} %pad_maximum_fusion.refs_2_), channel_id=1, source_target_pairs={{0,64},{1,5},{2,66},{3,7},{4,68},{5,1},{6,70},{7,3},{8,72},{9,13},... | collective-permute-start | bytes 3194888 | tf_op jit(solution)/shard_map/ppermute | solution.py:46
  19.3 1.3 collective-permute-start.5
  20.7 0.2 copy.44
  20.9 0.2 concatenate.12
  21.1 0.1 copy.46
  21.1 0.1 copy.43
  21.3 0.5 broadcast.71
  21.8 0.7 reduce.3
  22.4 0.1 lt.69
  22.6 0.1 compare_select_fusion
  22.7 0.1 copy.45
  22.8 0.1 rev.6
  23.0 0.7 copy.49
  23.7 7.9 %all-to-all-start = ((s32[64,1,128]{2,1,0:T(1,128)}), s32[64,1,128]{2,1,0:T(1,128)S(1)}, u32[]{:S(2)}, u32[]{:S(2)}) async-start(s32[64,1,128]{2,1,0:T(1,128)} %copy.49), calls=%async_computation | async-start | bytes 65536 | tf_op jit(solution)/shard_map/all_to_all | solution.py:300
  31.5 0.1 pad_add_fusion.1.refs_0_.here
  31.6 15.8 %all-to-all-done = s32[64,1,128]{2,1,0:T(1,128)S(1)} async-done(((s32[64,1,128]{2,1,0:T(1,128)}), s32[64,1,128]{2,1,0:T(1,128)S(1)}, u32[]{:S(2)}, u32[]{:S(2)}) %all-to-all-start) | async-done | bytes 32800 | tf_op jit(solution)/shard_map/all_to_all | solution.py:300
  47.5 0.0 collective-permute-done.3.refs_3_
  47.5 0.0 collective-permute-done.4.refs_4_
  47.5 0.0 collective-permute-done.5.refs_5_
  47.5 5.9 %shard_map.86 = (bf16[128,64,128]{2,1,0:T(8,128)(2,1)}, bf16[128,64,128]{2,1,0:T(8,128)(2,1)}) custom-call(s32[4]{0:T(128)S(1)} %pad_add_fusion.1.refs_0_.here, s32[64,128]{1,0:T(8,128)S(1)} %bitcast.24, bf16[4,1040,128]{2,1,0:T(8,128)(2,1)S(1)} %pad_maximum_fusion.refs_2_, bf16[4,1040,128]{2,1,0:T(8,128)(2,1)S(1)} %collective-permute-done.3.refs_3_, ...), custom_call_target="tpu_custom_call" | custom-call | bytes 14000000 | tf_op jit(solution)/shard_map/pallas_call | solution.py:97
  53.4 0.9 collective-permute-start.9
  54.3 2.4 %collective-permute-start.10 = (bf16[128,64,128]{2,1,0:T(8,128)(2,1)}, bf16[128,64,128]{2,1,0:T(8,128)(2,1)}, u32[]{:S(2)}, u32[]{:S(2)}) collective-permute-start(bf16[128,64,128]{2,1,0:T(8,128)(2,1)} %get-tuple-element.19), channel_id=1, source_target_pairs={{0,6},{1,25},{2,0},{3,27},{4,2},{5,29},{6,4},{7,31},{8,14},{9,1},{... | collective-permute-start | bytes 6291464 | tf_op jit(solution)/shard_map/ppermute | solution.py:46
  56.7 3.8 %shard_map.87 = (bf16[128,64,128]{2,1,0:T(8,128)(2,1)S(1)}, bf16[128,64,128]{2,1,0:T(8,128)(2,1)S(1)}) custom-call(s32[4]{0:T(128)S(1)} %pad_add_fusion.1.refs_0_.here, bf16[128,64,128]{2,1,0:T(8,128)(2,1)} %get-tuple-element.12.refs_1_, bf16[4,1040,128]{2,1,0:T(8,128)(2,1)S(1)} %pad_maximum_fusion.refs_2_, ...), custom_call_target="tpu_custom_call" | custom-call | bytes 14000000 | tf_op jit(solution)/shard_map/pallas_call | solution.py:97
  60.5 1.3 copy-done.2
  61.8 1.3 copy-done.8
  63.1 22.1 %shard_map.88 = (s32[3202]{0:T(1024)}, s32[3202]{0:T(1024)}) custom-call(s32[4]{0:T(128)} %copy-done.7, s32[8192]{0:T(1024)} %bitcast.25, bf16[128,64,128]{2,1,0:T(8,128)(2,1)} %copy-done.2), custom_call_target="tpu_custom_call" | custom-call | bytes 35000000 | tf_op jit(solution)/shard_map/pallas_call | solution.py:181
  85.3 0.3 collective-permute-start.7
  85.6 0.0 collective-permute-start.6
  85.6 0.1 copy.42
  85.7 0.2 iota_compare_fusion.1
  86.0 0.1 copy.54
  86.1 0.6 collective-permute-done.6
  86.8 0.0 copy-start
  86.8 2.8 %copy-done = bf16[128,192,128]{2,1,0:T(8,128)(2,1)S(1)} copy-done((bf16[128,192,128]{2,1,0:T(8,128)(2,1)S(1)}, bf16[128,192,128]{2,1,0:T(8,128)(2,1)}, u32[]{:S(2)}) %copy-start) | copy-done | bytes 6291480
  89.6 0.7 copy-done.6
  90.3 12.9 %shard_map.89.refs_5_ = f32[64,32]{1,0:T(8,128)S(1)} custom-call(s32[3202]{0:T(1024)S(1)} %copy-done.6, s32[256]{0:T(256)S(1)} %constant_dynamic-update-slice_fusion.refs_1_, bf16[128,64,128]{2,1,0:T(8,128)(2,1)S(1)} %copy-done.3, bf16[128,64,128]{2,1,0:T(8,128)(2,1)} %collective-permute-done.9.refs_3_, ...), custom_call_target="tpu_custom_call" | custom-call | bytes 42000000 | tf_op jit(solution)/shard_map/pallas_call | solution.py:268
  103.1 10.0 %collective-permute-done.7.refs_2_ = bf16[128,64,128]{2,1,0:T(8,128)(2,1)} collective-permute-done((bf16[128,64,128]{2,1,0:T(8,128)(2,1)}, bf16[128,64,128]{2,1,0:T(8,128)(2,1)}, u32[]{:S(2)}, u32[]{:S(2)}) %collective-permute-start.7) | collective-permute-done | bytes 2097184 | tf_op jit(solution)/shard_map/ppermute | solution.py:46
  113.2 7.6 %shard_map.90 = f32[64,32]{1,0:T(8,128)} custom-call(s32[3202]{0:T(1024)S(1)} %copy-done.5, s32[256]{0:T(256)S(1)} %constant_dynamic-update-slice_fusion.refs_1_, bf16[128,64,128]{2,1,0:T(8,128)(2,1)} %collective-permute-done.7.refs_2_, bf16[128,192,128]{2,1,0:T(8,128)(2,1)S(1)} %copy-done.1, bf16[128,192,128]{2,1,0:T(8,128)(2,1)} %collective-permute-done.8.refs_6_.refs_4_, ...), custom_call_target="tpu_custom_call" | custom-call | bytes 28000000 | tf_op jit(solution)/shard_map/pallas_call | solution.py:268
  120.8 10.8 %all-to-all-start.1 = ((f32[64,1,32]{2,1,0:T(1,128)}), f32[64,1,32]{2,1,0:T(1,128)S(1)}, u32[]{:S(2)}, u32[]{:S(2)}) async-start(f32[64,1,32]{2,1,0:T(1,128)} %bitcast.16), calls=%async_computation.1 | async-start | bytes 65536 | tf_op jit(solution)/shard_map/all_to_all | solution.py:314
  131.5 0.1 and_reduce_fusion
  131.7 9.4 %all-to-all-done.1 = f32[64,1,32]{2,1,0:T(1,128)S(1)} async-done(((f32[64,1,32]{2,1,0:T(1,128)}), f32[64,1,32]{2,1,0:T(1,128)S(1)}, u32[]{:S(2)}, u32[]{:S(2)}) %all-to-all-start.1) | async-done | bytes 8224 | tf_op jit(solution)/shard_map/all_to_all | solution.py:314
  141.1 0.1 copy.51
  141.2 0.1 copy.52
  141.3 0.2 reshape.106
  141.5 0.2 reshape.105
  141.7 0.2 broadcast_select_fusion
  141.9 0.1 copy.56
  142.0 0.2 fusion.3
  142.1 0.2 fusion.2
  142.4 0.7 copy.57
  143.1 0.5 broadcast_select_fusion.2
  (37 shorter events, 0.2 us)
Async XLA Ops:
  0.6 86.1 %collective-permute-start.8 = (bf16[128,192,128]{2,1,0:T(8,128)(2,1)}, bf16[128,192,128]{2,1,0:T(8,128)(2,1)}, u32[]{:S(2)}, u32[]{:S(2)}) collective-permute-start(bf16[128,192,128]{2,1,0:T(8,128)(2,1)} %refs_3_.1), channel_id=1, source_target_pairs={{0,1},{1,0},{2,3},{3,2},{4,5},{5,4},{6,7},{7,6},{8,9},{9,8},{10,11... | collective-permute-start | bytes 18874376 | tf_op jit(solution)/shard_map/ppermute | solution.py:303
  2.7 8.0 %collective-permute-start.1 = (bf16[1040,128]{1,0:T(8,128)(2,1)S(1)}, bf16[1040,128]{1,0:T(8,128)(2,1)S(1)}, u32[]{:S(2)}, u32[]{:S(2)}) collective-permute-start(bf16[1040,128]{1,0:T(8,128)(2,1)S(1)} %get-tuple-element.27), channel_id=1, source_target_pairs={{0,16},{1,65},{2,18},{3,67},{4,20},{5,69},{6,22},{7,71},{8,24},{9,... | collective-permute-start | bytes 798728 | tf_op jit(solution)/shard_map/ppermute | solution.py:46
  5.9 7.9 %collective-permute-start.2 = (bf16[1040,128]{1,0:T(8,128)(2,1)S(1)}, bf16[1040,128]{1,0:T(8,128)(2,1)S(1)}, u32[]{:S(2)}, u32[]{:S(2)}) collective-permute-start(bf16[1040,128]{1,0:T(8,128)(2,1)S(1)} %get-tuple-element.27), channel_id=1, source_target_pairs={{0,24},{1,97},{2,26},{3,99},{4,28},{5,101},{6,30},{7,103},{8,0},{9... | collective-permute-start | bytes 798728 | tf_op jit(solution)/shard_map/ppermute | solution.py:46
  7.0 7.6 %collective-permute-start = (bf16[1040,128]{1,0:T(8,128)(2,1)S(1)}, bf16[1040,128]{1,0:T(8,128)(2,1)S(1)}, u32[]{:S(2)}, u32[]{:S(2)}) collective-permute-start(bf16[1040,128]{1,0:T(8,128)(2,1)S(1)} %get-tuple-element.27), channel_id=1, source_target_pairs={{0,8},{1,33},{2,10},{3,35},{4,12},{5,37},{6,14},{7,39},{8,16},{9,4... | collective-permute-start | bytes 798728 | tf_op jit(solution)/shard_map/ppermute | solution.py:46
  14.7 6.0 %copy-start.9 = (s32[1,128,4,4]{1,3,2,0:T(4,128)S(1)}, s32[1,128,4,4]{1,3,2,0:T(4,128)}, u32[]{:S(2)}) copy-start(s32[1,128,4,4]{1,3,2,0:T(4,128)} %param.12) | copy-start | bytes 24580
  14.7 6.5 %copy-start.10 = (s32[1,128,4]{1,2,0:T(4,128)S(1)}, s32[1,128,4]{1,2,0:T(4,128)}, u32[]{:S(2)}) copy-start(s32[1,128,4]{1,2,0:T(4,128)} %param.13) | copy-start | bytes 6148
  14.7 7.1 %copy-start.12 = (s32[1,128]{1,0:T(1,128)S(1)}, s32[1,128]{1,0:T(1,128)}, u32[]{:S(2)}) copy-start(s32[1,128]{1,0:T(1,128)} %param.11) | copy-start | bytes 1540
  14.8 32.7 %collective-permute-start.3 = (bf16[4,1040,128]{2,1,0:T(8,128)(2,1)S(1)}, bf16[4,1040,128]{2,1,0:T(8,128)(2,1)S(1)}, u32[]{:S(2)}, u32[]{:S(2)}) collective-permute-start(bf16[4,1040,128]{2,1,0:T(8,128)(2,1)S(1)} %pad_maximum_fusion.refs_2_), channel_id=1, source_target_pairs={{0,32},{1,3},{2,34},{3,5},{4,36},{5,7},{6,38},{7,1},{8,40},{9,11},... | collective-permute-start | bytes 3194888 | tf_op jit(solution)/shard_map/ppermute | solution.py:46
  16.4 31.0 %collective-permute-start.4 = (bf16[4,1040,128]{2,1,0:T(8,128)(2,1)S(1)}, bf16[4,1040,128]{2,1,0:T(8,128)(2,1)S(1)}, u32[]{:S(2)}, u32[]{:S(2)}) collective-permute-start(bf16[4,1040,128]{2,1,0:T(8,128)(2,1)S(1)} %pad_maximum_fusion.refs_2_), channel_id=1, source_target_pairs={{0,64},{1,5},{2,66},{3,7},{4,68},{5,1},{6,70},{7,3},{8,72},{9,13},... | collective-permute-start | bytes 3194888 | tf_op jit(solution)/shard_map/ppermute | solution.py:46
  19.3 28.2 %collective-permute-start.5 = (bf16[4,1040,128]{2,1,0:T(8,128)(2,1)S(1)}, bf16[4,1040,128]{2,1,0:T(8,128)(2,1)}, u32[]{:S(2)}, u32[]{:S(2)}) collective-permute-start(bf16[4,1040,128]{2,1,0:T(8,128)(2,1)S(1)} %pad_maximum_fusion.refs_2_), channel_id=1, source_target_pairs={{0,96},{1,7},{2,98},{3,1},{4,100},{5,3},{6,102},{7,5},{8,104},{9,1... | collective-permute-start | bytes 3194888 | tf_op jit(solution)/shard_map/ppermute | solution.py:46
  23.7 23.8 %all-to-all-start = ((s32[64,1,128]{2,1,0:T(1,128)}), s32[64,1,128]{2,1,0:T(1,128)S(1)}, u32[]{:S(2)}, u32[]{:S(2)}) async-start(s32[64,1,128]{2,1,0:T(1,128)} %copy.49), calls=%async_computation | async-start | bytes 65536 | tf_op jit(solution)/shard_map/all_to_all | solution.py:300
  31.6 25.1 %copy-start.7 = (s32[4]{0:T(128)}, s32[4]{0:T(128)S(1)}, u32[]{:S(2)}) copy-start(s32[4]{0:T(128)S(1)} %pad_add_fusion.1.refs_0_.here) | copy-start | bytes 52
  47.5 5.9 %copy-start.4 = (s32[64,1,128]{2,1,0:T(1,128)}, s32[64,1,128]{2,1,0:T(1,128)S(1)}, u32[]{:S(2)}) copy-start(s32[64,1,128]{2,1,0:T(1,128)S(1)} %all-to-all-done) | copy-start | bytes 98308
  53.4 33.4 %collective-permute-start.9 = (bf16[128,64,128]{2,1,0:T(8,128)(2,1)}, bf16[128,64,128]{2,1,0:T(8,128)(2,1)}, u32[]{:S(2)}, u32[]{:S(2)}) collective-permute-start(bf16[128,64,128]{2,1,0:T(8,128)(2,1)} %get-tuple-element.12.refs_1_), channel_id=1, source_target_pairs={{0,2},{1,9},{2,4},{3,11},{4,6},{5,13},{6,0},{7,15},{8,10},{9,17},{... | collective-permute-start | bytes 6291464 | tf_op jit(solution)/shard_map/ppermute | solution.py:46
  54.3 32.4 %collective-permute-start.10 = (bf16[128,64,128]{2,1,0:T(8,128)(2,1)}, bf16[128,64,128]{2,1,0:T(8,128)(2,1)}, u32[]{:S(2)}, u32[]{:S(2)}) collective-permute-start(bf16[128,64,128]{2,1,0:T(8,128)(2,1)} %get-tuple-element.19), channel_id=1, source_target_pairs={{0,6},{1,25},{2,0},{3,27},{4,2},{5,29},{6,4},{7,31},{8,14},{9,1},{... | collective-permute-start | bytes 6291464 | tf_op jit(solution)/shard_map/ppermute | solution.py:46
  60.5 1.3 copy-start.2
  61.8 1.3 copy-start.8
  63.1 22.5 %copy-start.13 = (s32[128]{0:T(128)S(1)}, s32[128]{0:T(128)}, u32[]{:S(2)}) copy-start(s32[128]{0:T(128)} %param.9) | copy-start | bytes 1540
  63.1 22.6 %copy-start.11 = (s32[1,128,4]{1,2,0:T(4,128)S(1)}, s32[1,128,4]{1,2,0:T(4,128)}, u32[]{:S(2)}) copy-start(s32[1,128,4]{1,2,0:T(4,128)} %param.10) | copy-start | bytes 6148
  63.1 23.6 %copy-start.3 = (bf16[128,64,128]{2,1,0:T(8,128)(2,1)S(1)}, bf16[128,64,128]{2,1,0:T(8,128)(2,1)}, u32[]{:S(2)}) copy-start(bf16[128,64,128]{2,1,0:T(8,128)(2,1)} %copy-done.2) | copy-start | bytes 6291460
  85.3 27.9 %collective-permute-start.7 = (bf16[128,64,128]{2,1,0:T(8,128)(2,1)}, bf16[128,64,128]{2,1,0:T(8,128)(2,1)}, u32[]{:S(2)}, u32[]{:S(2)}) collective-permute-start(bf16[128,64,128]{2,1,0:T(8,128)(2,1)} %copy-done.8), channel_id=1, source_target_pairs={{0,4},{1,17},{2,6},{3,19},{4,0},{5,21},{6,2},{7,23},{8,12},{9,25},... | collective-permute-start | bytes 6291464 | tf_op jit(solution)/shard_map/ppermute | solution.py:46
  85.6 1.1 collective-permute-start.6
  86.8 2.8 %copy-start = (bf16[128,192,128]{2,1,0:T(8,128)(2,1)S(1)}, bf16[128,192,128]{2,1,0:T(8,128)(2,1)}, u32[]{:S(2)}) copy-start(bf16[128,192,128]{2,1,0:T(8,128)(2,1)} %refs_3_.1) | copy-start | bytes 18874372
  89.6 0.7 copy-start.6
  90.3 22.9 %copy-start.1 = (bf16[128,192,128]{2,1,0:T(8,128)(2,1)S(1)}, bf16[128,192,128]{2,1,0:T(8,128)(2,1)}, u32[]{:S(2)}) copy-start(bf16[128,192,128]{2,1,0:T(8,128)(2,1)} %refs_3_.1) | copy-start | bytes 18874372
  90.3 22.9 %copy-start.5 = (s32[3202]{0:T(1024)S(1)}, s32[3202]{0:T(1024)}, u32[]{:S(2)}) copy-start(s32[3202]{0:T(1024)} %get-tuple-element.14.refs_0_) | copy-start | bytes 38428
  120.8 20.3 %all-to-all-start.1 = ((f32[64,1,32]{2,1,0:T(1,128)}), f32[64,1,32]{2,1,0:T(1,128)S(1)}, u32[]{:S(2)}, u32[]{:S(2)}) async-start(f32[64,1,32]{2,1,0:T(1,128)} %bitcast.16), calls=%async_computation.1 | async-start | bytes 65536 | tf_op jit(solution)/shard_map/all_to_all | solution.py:314

commit v3 on v2

v3 whole, which is shorter than its diff:
```python
import itertools

import jax
import jax.numpy as jnp
from jax import lax
from jax.experimental import pallas as pl
from jax.experimental.pallas import tpu as pltpu
from jax.sharding import Mesh, PartitionSpec as P

ALL = ("y", "x", "z", "core")
PLACE = ("y", "x", "z")
SIDE = 4
CHIPS = SIDE**3
EARLY = CHIPS * 3 // 4
CAPS = 4
SLOTS = 4
LANE = 4
UNROLL = 16
NOBODY = EARLY * 2 * SLOTS * CAPS
MIB = 1 << 20
CONTS = 16
NOTE_ROWS = 16
NOTES = 32
PASSAGES = 128

ORDERS = (("x", "y", "z"), ("y", "z", "x"))


def smem():
    return pl.BlockSpec(memory_space=pltpu.SMEM)


def vmem():
    return pl.BlockSpec(memory_space=pltpu.VMEM)


def hbm():
    return pl.BlockSpec(memory_space=pl.ANY)


def shift(array, stage, by):
    pairs = []
    for y, x, z, core in itertools.product(range(SIDE), range(SIDE), range(SIDE), range(2)):
        at = {"y": y, "x": x, "z": z}
        axis = ORDERS[core][stage]
        to = dict(at, **{axis: (at[axis] + by) % SIDE})
        pairs.append(tuple(((p["y"] * SIDE + p["x"]) * SIDE + p["z"]) * 2 + core for p in (at, to)))
    return lax.ppermute(array, ALL, pairs)


def cost(us):
    return pl.CostEstimate(flops=0, bytes_accessed=int(us * 3_500_000), transcendentals=0)


def chip_low(at, low):
    y, x, z = ((at[k] - low[k]) & (SIDE - 1) for k in "yxz")
    return (y * SIDE + x) * SIDE + z


def by_core(core, digits):
    low = [dict(zip(order, digits)) for order in ORDERS]
    return {k: jnp.where(core == 0, low[0][k], low[1][k]) for k in "yxz"}


def select_kernel(targets, here, after, *refs):
    *planes, table, notes, arrived = refs
    planes, outs = planes[: -len(targets)], planes[-len(targets) :]
    at, core = dict(zip("yxz", (here[0], here[1], here[2]))), here[3]
    end = planes[0].shape[1] - NOTE_ROWS
    tokens = end // CONTS
    for source in range(SIDE * len(planes)):
        told = planes[source // SIDE][source % SIDE, end : end + NOTE_ROWS, :]
        table[source] = told.astype(jnp.float32).astype(jnp.int32)[:8]
    copy = pltpu.make_async_copy(table, notes, arrived)
    copy.start()
    owners = []
    for third in targets:
        chip = chip_low(at, by_core(core, (0, 0, -third)))
        owners += [chip * 2 + core, chip * 2 + 1 - core]
    copy.wait()
    for second in range(len(planes)):

        def step(first, carry):
            source = second * SIDE + first
            for out, target in enumerate(outs):
                picked = []
                for slot in range(2 * SLOTS):
                    cont = notes[source, slot % SLOTS, owners[out * 2 + slot // SLOTS]]
                    rows = pl.ds(pl.multiple_of(cont * tokens, 16), tokens)
                    picked.append(planes[second][first, rows, :])
                for slot, rows in enumerate(picked):
                    target[source * 2 * SLOTS + slot] = rows
            return carry

        lax.fori_loop(0, SIDE, step, 0)


def select(targets, here, after, planes):
    tokens = (planes[0].shape[1] - NOTE_ROWS) // CONTS
    sources = SIDE * len(planes)
    shape = (sources * 2 * SLOTS, tokens, planes[0].shape[2])
    return pl.pallas_call(
        lambda *refs: select_kernel(targets, *refs),
        out_shape=[jax.ShapeDtypeStruct(shape, planes[0].dtype)] * len(targets),
        in_specs=[smem(), hbm()] + [vmem()] * len(planes),
        out_specs=[vmem()] * len(targets),
        cost_estimate=cost(4),
        scratch_shapes=[
            pltpu.VMEM((sources, 8, 128), jnp.int32),
            pltpu.SMEM((sources, 8, 128), jnp.int32),
            pltpu.SemaphoreType.DMA(()),
        ],
        compiler_params=pltpu.CompilerParams(vmem_limit_bytes=14 * MIB),
    )(here, after, *planes)


def room(part):
    sources = (EARLY, CHIPS - EARLY)[part]
    most = (sources * SLOTS * CAPS + (LANE - 1) * PASSAGES) // LANE
    return -(-most // 32) * 32


def start_of(part, which):
    before = 2 * sum(room(p) for p in range(part))
    return (before + (room(part) * which if which else 0)) * LANE


def group_kernel(here, notes, held, lists, passed, blank, table, spots, arrived):
    rows, lanes = lists.shape
    counts_row = rows - 8
    dump = counts_row * lanes + lanes // 2
    core = here[3]
    source = lax.broadcasted_iota(jnp.int32, (CHIPS, 1), 0)
    far_y = (here[0] - (source >> 4)) & (SIDE - 1)
    far_x = (here[1] - (source >> 2)) & (SIDE - 1)
    far_z = (here[2] - source) & (SIDE - 1)
    first = jnp.where(core == 0, far_x, far_y)
    second = jnp.where(core == 0, far_y, far_z)
    third = jnp.where(core == 0, far_z, far_x)
    late = third == 2
    third = jnp.where(late, 0, jnp.where(third == 3, 2, third))
    local = (third * SIDE + second) * SIDE + first
    shift_late = jnp.where(late, PASSAGES, 0)

    lane = lax.broadcasted_iota(jnp.int32, (CHIPS, lanes), 1)
    key = lax.broadcasted_iota(jnp.int32, (CHIPS, 2 * PASSAGES), 1)
    square = (CHIPS, CHIPS)
    earlier = lax.broadcasted_iota(jnp.int32, square, 1) < lax.broadcasted_iota(jnp.int32, square, 0)
    earlier = earlier.astype(jnp.float32).astype(jnp.bfloat16)
    square = (PASSAGES, PASSAGES)
    below = lax.broadcasted_iota(jnp.int32, square, 0) < lax.broadcasted_iota(jnp.int32, square, 1)
    below = below.astype(jnp.float32).astype(jnp.bfloat16)
    data = notes[...]
    found = jnp.zeros((CHIPS, lanes), jnp.int32)
    counts = jnp.zeros((1, lanes), jnp.int32)
    lane_row = lax.broadcasted_iota(jnp.int32, (1, lanes), 1)

    for which in range(2):
        info = which * NOTES
        hits, ranks, lives = [], [], []
        many = jnp.zeros((1, 2 * PASSAGES), jnp.float32)
        for j in range(SLOTS):
            for k in range(CAPS):
                at = info + SLOTS + j * CAPS + k
                passage = data[:, at : at + 1]
                live = data[:, info + j : info + j + 1] > k
                hit = jnp.where(live & (passage + shift_late == key), 1.0, 0.0)
                ahead = jnp.dot(
                    earlier, hit.astype(jnp.bfloat16), preferred_element_type=jnp.float32
                )
                ranks.append(jnp.sum(hit * (ahead + many), axis=1, keepdims=True))
                many = many + jnp.sum(hit, axis=0, keepdims=True)
                hits.append(hit)
                lives.append(live)
                slot = local * (2 * SLOTS) + which * SLOTS + j
                code = (passage << 20) | (slot << 11) | (slot * CAPS + k)
                pair = (which * SLOTS + j) * CAPS + k
                found = jnp.where(lane == 32 + pair, code, found)
        groups = (many.astype(jnp.int32) + (LANE - 1)) // LANE
        starts = []
        for part in range(2):
            mine = groups[:, part * PASSAGES : (part + 1) * PASSAGES]
            wide = jnp.broadcast_to(mine.astype(jnp.float32), (16, PASSAGES)).astype(jnp.bfloat16)
            base = jnp.dot(wide, below, preferred_element_type=jnp.float32)[0:1]
            starts.append(base * LANE + start_of(part, which))
            total = jnp.sum(mine.astype(jnp.float32), axis=1, keepdims=True).astype(jnp.int32)
            counts = jnp.where(lane_row == part * 2 + which, total, counts)
        begin = jnp.concatenate(starts, axis=1)
        for i, (hit, rank, live) in enumerate(zip(hits, ranks, lives)):
            spot = jnp.sum(hit * begin, axis=1, keepdims=True) + rank
            spot = jnp.where(live, spot.astype(jnp.int32), dump)
            found = jnp.where(lane == which * SLOTS * CAPS + i, spot, found)

    table[...] = found
    blank[...] = jnp.full((rows, lanes), NOBODY, jnp.int32)
    blank[counts_row : counts_row + 1, :] = counts
    copies = [
        pltpu.make_async_copy(table, spots, arrived.at[0]),
        pltpu.make_async_copy(blank, lists, arrived.at[1]),
    ]
    for copy in copies:
        copy.start()
    for copy in copies:
        copy.wait()

    def scatter(source, carry):
        for pair in range(2 * SLOTS * CAPS):
            spot = spots[source, pair]
            lists[spot >> 7, spot & 127] = spots[source, 32 + pair]
        return carry

    lax.fori_loop(0, CHIPS, scatter, 0)


def group_pairs(here, notes, held):
    rows = start_of(2, 0) // 128 + 8
    rows = -(-rows // 8) * 8
    return pl.pallas_call(
        group_kernel,
        out_shape=(
            jax.ShapeDtypeStruct((rows, 128), jnp.int32),
            jax.ShapeDtypeStruct(held.shape, held.dtype),
        ),
        in_specs=[smem(), vmem(), hbm()],
        out_specs=(smem(), hbm()),
        input_output_aliases={2: 1},
        scratch_shapes=[
            pltpu.VMEM((rows, 128), jnp.int32),
            pltpu.VMEM((CHIPS, 128), jnp.int32),
            pltpu.SMEM((CHIPS, 128), jnp.int32),
            pltpu.SemaphoreType.DMA((2,)),
        ],
        cost_estimate=cost(8),
        compiler_params=pltpu.CompilerParams(vmem_limit_bytes=16 * MIB),
    )(here, notes, held)


def score_kernel(part, many, here, lists, lengths, *refs):
    pieces, refs = refs[:many], refs[many:]
    own, sibling, refs = refs[0], refs[1], refs[2:]
    *refs, theirs, arrived, peaks = refs
    swap_in = pltpu.make_async_copy(sibling, theirs, arrived.at[many])
    *before, out, rows = refs
    each = pieces[0].shape[0]
    copies = [
        pltpu.make_async_copy(piece, rows.at[pl.ds(i * each, each)], arrived.at[i])
        for i, piece in enumerate(pieces)
    ]
    for copy in copies:
        copy.start()
    swap_in.start()
    peaks[...] = jnp.zeros_like(peaks)
    for copy in copies:
        copy.wait()

    sources = (EARLY, CHIPS - EARLY)[part]
    tokens = rows.shape[1]
    each = out.shape[1]
    pairs = sources * each
    lanes = lists.shape[1]
    lower = lax.broadcasted_iota(jnp.int32, (1, 2 * tokens), 1) < tokens
    token = lax.broadcasted_iota(jnp.int32, (own.shape[1], LANE * tokens), 0)
    for which, texts in enumerate((own, theirs)):
        if which == 1:
            swap_in.wait()
        start = start_of(part, which) // lanes

        def step(i, carry):
            line = start + i * (UNROLL * LANE) // lanes
            first = i * (UNROLL * LANE) % lanes
            for u in range(UNROLL):
                code = [lists[line, first + u * LANE + k] for k in range(LANE)]
                passage = code[0] >> 20
                similar = lax.dot_general(
                    texts[passage],
                    jnp.concatenate([rows[(c >> 11) & 511] for c in code], axis=0),
                    (((1,), (1,)), ((), ())),
                    preferred_element_type=jnp.float32,
                )
                inside = token < lengths[which * own.shape[0] + passage]
                top = jnp.max(jnp.where(inside, similar, -jnp.inf), axis=0, keepdims=True)
                for k in range(0, LANE, 2):
                    both = top[:, k * tokens : (k + 2) * tokens]
                    peaks[pl.ds(code[k] & 2047, 1), :] = jnp.where(lower, both, 0.0)
                    peaks[pl.ds(code[k + 1] & 2047, 1), :] = jnp.where(lower, 0.0, both)
            return carry

        steps = (lists[lists.shape[0] - 8, part * 2 + which] + UNROLL - 1) // UNROLL
        lax.fori_loop(0, steps, step, 0)
    high = peaks[0:pairs, :].astype(jnp.bfloat16)
    low = (peaks[0:pairs, :] - high.astype(jnp.float32)).astype(jnp.bfloat16)
    ones = jnp.ones((16, 2 * tokens), jnp.bfloat16)
    total = sum(
        lax.dot_general(
            ones, part, (((1,), (1,)), ((), ())), preferred_element_type=jnp.float32
        )
        for part in (high, low)
    )
    total = total[0:1] * (1.0 / tokens)
    if before:
        out[...] = before[0][...]
    at, core = dict(zip("yxz", (here[0], here[1], here[2]))), here[3]
    for source in range(sources):
        third = (0, 1, 3)[source // (SIDE * SIDE)] if part == 0 else 2
        digits = (source % SIDE, source // SIDE % SIDE, third)
        chip = chip_low(at, by_core(core, digits))
        out[pl.ds(chip, 1), :] = total[:, source * each : (source + 1) * each]


def score(here, lists, lengths, pieces, own, sibling, before=()):
    pairs = CHIPS * 2 * SLOTS * CAPS
    many = len(pieces)
    tokens = pieces[0].shape[1]
    part = len(before)
    piece = pieces[0].shape
    scratch = [
        pltpu.VMEM((many * piece[0],) + piece[1:], own.dtype),
        pltpu.VMEM(sibling.shape, sibling.dtype),
        pltpu.SemaphoreType.DMA((many + 1,)),
        pltpu.VMEM((NOBODY + 8, 2 * tokens), jnp.float32),
    ]
    return pl.pallas_call(
        lambda *refs: score_kernel(part, many, *refs),
        out_shape=jax.ShapeDtypeStruct((CHIPS, pairs // CHIPS), jnp.float32),
        in_specs=[smem()] * 3
        + [hbm()] * many
        + [vmem(), hbm()]
        + [vmem()] * len(before),
        out_specs=vmem(),
        scratch_shapes=scratch,
        cost_estimate=cost(8 if before else 12),
        compiler_params=pltpu.CompilerParams(vmem_limit_bytes=(26 if before else 56) * MIB),
    )(here, lists, lengths, *pieces, own, sibling, *before)


def of_owner(here, which):
    chip = lax.broadcasted_iota(jnp.int32, (CHIPS, 2 * CHIPS), 0)
    device = lax.broadcasted_iota(jnp.int32, (CHIPS, 2 * CHIPS), 1)
    core = here[3] if which == 0 else 1 - here[3]
    return jnp.where(device == chip * 2 + core, 1.0, 0.0)


def used_caps(send_count, cand_count):
    slot = lax.broadcasted_iota(jnp.int32, cand_count.shape, 0)
    return jnp.where(slot < send_count, cand_count, 0)


def tell_kernel(here, send_count, cand_count, cand, out):
    used = used_caps(send_count[...], cand_count[...]).astype(jnp.float32)
    rest = jnp.zeros((NOTES - used.shape[0] - cand.shape[0], used.shape[1]), jnp.float32)
    told = jnp.concatenate([used, cand[...].astype(jnp.float32), rest], axis=0)
    told = told.astype(jnp.bfloat16)
    out[...] = jnp.zeros_like(out)
    for which in range(2):
        note = lax.dot_general(
            of_owner(here, which).astype(jnp.bfloat16),
            told,
            (((1,), (1,)), ((), ())),
            preferred_element_type=jnp.float32,
        )
        out[:, which * NOTES : (which + 1) * NOTES] = note.astype(jnp.int32)


def tell(here, send_count, cand_count, cand, after):
    return pl.pallas_call(
        lambda here, after, *refs: tell_kernel(here, *refs),
        out_shape=jax.ShapeDtypeStruct((CHIPS, 128), jnp.int32),
        in_specs=[smem(), hbm(), vmem(), vmem(), vmem()],
        out_specs=vmem(),
        cost_estimate=cost(1),
    )(here, after, send_count, cand_count, cand)


def finish_kernel(here, returned, send_count, cand_count, conts, scores, best):
    each = SLOTS * CAPS
    values = sum(
        lax.dot_general(
            returned[:, which * each : (which + 1) * each],
            of_owner(here, which),
            (((0,), (0,)), ((), ())),
            precision=lax.Precision.HIGHEST,
            preferred_element_type=jnp.float32,
        )
        for which in range(2)
    )
    used = used_caps(send_count[...], cand_count[...])
    lanes = values.shape[1]
    cap = lax.broadcasted_iota(jnp.int32, (CAPS, lanes), 0)
    cont = lax.broadcasted_iota(jnp.int32, (CONTS, lanes), 0)
    tops = jnp.full((CONTS, lanes), -jnp.inf, jnp.float32)
    for j in range(SLOTS):
        value = values[j * CAPS : (j + 1) * CAPS]
        live = cap < used[j : j + 1]
        scores[j * CAPS : (j + 1) * CAPS, :] = jnp.where(live, value, 0.0)
        top = jnp.max(jnp.where(live, value, -jnp.inf), axis=0, keepdims=True)
        tops = jnp.maximum(tops, jnp.where(conts[j : j + 1, :] == cont, top, -jnp.inf))
    top = jnp.max(tops, axis=1, keepdims=True)
    top = jnp.where(top > -jnp.inf, top, 0.0)
    best[...] = jnp.broadcast_to(top, (CONTS, lanes)).T[0:1]


def finish(here, returned, send_count, cand_count, conts):
    devices = 2 * CHIPS
    return pl.pallas_call(
        finish_kernel,
        out_shape=(
            jax.ShapeDtypeStruct((SLOTS * CAPS, devices), jnp.float32),
            jax.ShapeDtypeStruct((1, CONTS), jnp.float32),
        ),
        in_specs=[smem()] + [vmem()] * 4,
        out_specs=(vmem(), vmem()),
        cost_estimate=cost(2),
    )(here, returned, send_count, cand_count, conts)


def body(queries, passages, pass_len, send_cont, send_count, cand, cand_count):
    here = jnp.stack([lax.axis_index(k) for k in ALL]).astype(jnp.int32)
    conts = send_cont[0].T
    counts = cand_count[0].T
    chosen = cand[0].transpose(1, 2, 0).reshape(SLOTS * CAPS, -1)

    told = jnp.pad(conts.astype(queries.dtype), ((0, NOTE_ROWS - SLOTS), (0, 0)))
    piece = jnp.concatenate([queries.reshape(-1, queries.shape[2]), told], axis=0)
    line = jnp.stack([piece] + [shift(piece, 0, by) for by in range(1, SIDE)])
    planes = [line] + [shift(line, 1, by) for by in range(1, SIDE)]
    notes = tell(here, send_count, counts, chosen, line)
    notes = lax.all_to_all(notes, PLACE, split_axis=0, concat_axis=0, tiled=True)

    swap = [(0, 1), (1, 0)]
    sibling = lax.ppermute(passages, "core", swap)
    lengths = jnp.concatenate([pass_len, lax.ppermute(pass_len, "core", swap)])

    halves = [
        select(range(SIDE), here, here, planes[:2]),
        select(range(SIDE), here, notes, planes[2:]),
    ]
    near = [shift(half[1], 2, 1) for half in halves]
    back = [shift(half[3], 2, 3) for half in halves]
    lists, across = group_pairs(here, notes, halves[1][2])
    far = [shift(halves[0][2], 2, 2), shift(across, 2, 2)]
    around = [half[0] for half in halves] + near + back
    handled = score(here, lists, lengths, around, passages, sibling)
    handled = score(here, lists, lengths, far, passages, sibling, (handled,))
    returned = lax.all_to_all(handled, PLACE, split_axis=0, concat_axis=0, tiled=True)
    scores, best = finish(here, returned, send_count, counts, conts)
    scores = scores.reshape(1, SLOTS, CAPS, -1).transpose(0, 3, 1, 2)
    return scores, best.reshape(-1)


def solution(mesh):
    mesh = Mesh(mesh.devices.reshape(SIDE, SIDE, SIDE, 2), ALL)
    in_specs = (
        P(ALL, None, None),
        P(ALL, None, None),
        P(ALL),
        P(ALL, None, None),
        P(ALL, None),
        P(ALL, None, None, None),
        P(ALL, None, None),
    )
    out_specs = (P(ALL, None, None, None), P(ALL))
    return jax.shard_map(body, mesh=mesh, in_specs=in_specs, out_specs=out_specs, check_vma=False)
```

time: 144 us -> 139 us (0.965)
  waiting for transfers between devices: 42.7 us -> 21.5 us
  blocking collectives: 0 us -> 20.8 us
  local copies, waits for them, and re-layouts: 10.1 us -> 6.57 us
  other arithmetic: 4.22 us -> 2.46 us
  Pallas kernels: 52.2 us -> 53.9 us
    all_to_all x0 -> x1, blocking collectives: none -> 20.8 us  [body(): lax.all_to_all(handled, PLACE, split_axis=0, concat_axis=0, tiled=True)]
    all_to_all x2 -> x1, waiting for transfers between devices: 25.3 us -> 11.5 us  [body(): lax.all_to_all(notes, PLACE, split_axis=0, concat_axis=0, tiled=True)]
    all_to_all x2 -> x1, starting transfers between devices: 18.7 us -> 11.1 us  [body(): lax.all_to_all(notes, PLACE, split_axis=0, concat_axis=0, tiled=True)]
    ppermute x9 -> x12, starting transfers between devices: 14.8 us -> 21.8 us  [shift(): return lax.ppermute(array, ALL, pairs)]
    ppermute x9 -> x12, waiting for transfers between devices: 16.8 us -> 9.92 us  [shift(): return lax.ppermute(array, ALL, pairs)]
    pallas_call x3 -> x5, Pallas kernels: 42.5 us -> 46 us  [the longest x2 24.6 us: score(): pl.pallas_call(lambda *refs: score_kernel(part, many, *refs), out_shape=j...]
    pallas_call x2, Pallas kernels: 9.67 us -> 7.94 us  [select(): pl.pallas_call(lambda *refs: select_kernel(targets, *refs), out_shape=[ja...]
  transfers between devices with their start and end apart: 13 -> 15, of which waited for: 7 -> 5; matrix products, arithmetic and copies ran while one was open for 4% -> 2% of each run, Pallas kernels for 31% -> 32%
where the time goes in v3:
time: 139 us
  Pallas kernels  53.9 us (39%)
  starting transfers between devices  33 us (24%)
  waiting for transfers between devices  21.5 us (15%)
  blocking collectives  20.8 us (15%)
  local copies, waits for them, and re-layouts  6.57 us (5%)
  other arithmetic  2.46 us (2%)
    pallas_call x2, Pallas kernels, score(): pl.pallas_call(lambda *refs: score_kernel(part, many, *refs), out_shape=j...  24.6 us
    ppermute x12, starting transfers between devices, shift(): return lax.ppermute(array, ALL, pairs)  21.8 us
    all_to_all x1, blocking collectives, body(): lax.all_to_all(handled, PLACE, split_axis=0, concat_axis=0, tiled=True)  20.8 us
    pallas_call x1, Pallas kernels, group_pairs(): pl.pallas_call(group_kernel, out_shape=(jax.ShapeDtypeStruct((rows, 128),...  18 us
    all_to_all x1, waiting for transfers between devices, body(): lax.all_to_all(notes, PLACE, split_axis=0, concat_axis=0, tiled=True)  11.5 us
    all_to_all x1, starting transfers between devices, body(): lax.all_to_all(notes, PLACE, split_axis=0, concat_axis=0, tiled=True)  11.1 us
    ppermute x12, waiting for transfers between devices, shift(): return lax.ppermute(array, ALL, pairs)  9.92 us
    pallas_call x2, Pallas kernels, select(): pl.pallas_call(lambda *refs: select_kernel(targets, *refs), out_shape=[ja...  7.94 us
  transfers between devices with their start and end apart: 15, of which 5 were waited for; matrix products, arithmetic and copies ran while one was open for 2% of the time, Pallas kernels for 32%

profile of v3, /device:TPU:0, one launch (start us, length us, event | category | flops | bytes accessed | tf_op | source)
XLA Modules:
  0.0 139.0 jit_solution(15543588718179260631)
XLA Ops:
  0.6 0.1 collective-permute-start.9
  0.7 0.7 bitcast_convert_fusion
  1.4 1.0 fusion.2
  2.4 3.2 %collective-permute-start.1 = (bf16[1040,128]{1,0:T(8,128)(2,1)S(1)}, bf16[1040,128]{1,0:T(8,128)(2,1)S(1)}, u32[]{:S(2)}, u32[]{:S(2)}) collective-permute-start(bf16[1040,128]{1,0:T(8,128)(2,1)S(1)} %get-tuple-element.27), channel_id=1, source_target_pairs={{0,16},{1,65},{2,18},{3,67},{4,20},{5,69},{6,22},{7,71},{8,24},{9,... | collective-permute-start | bytes 798728 | tf_op jit(solution)/shard_map/ppermute | solution.py:48
  5.6 0.6 collective-permute-start
  6.2 2.6 %collective-permute-start.2 = (bf16[1040,128]{1,0:T(8,128)(2,1)S(1)}, bf16[1040,128]{1,0:T(8,128)(2,1)S(1)}, u32[]{:S(2)}, u32[]{:S(2)}) collective-permute-start(bf16[1040,128]{1,0:T(8,128)(2,1)S(1)} %get-tuple-element.27), channel_id=1, source_target_pairs={{0,24},{1,97},{2,26},{3,99},{4,28},{5,101},{6,30},{7,103},{8,0},{9... | collective-permute-start | bytes 798728 | tf_op jit(solution)/shard_map/ppermute | solution.py:48
  8.9 1.6 %collective-permute-done.1 = bf16[1040,128]{1,0:T(8,128)(2,1)S(1)} collective-permute-done((bf16[1040,128]{1,0:T(8,128)(2,1)S(1)}, bf16[1040,128]{1,0:T(8,128)(2,1)S(1)}, u32[]{:S(2)}, u32[]{:S(2)}) %collective-permute-start.1) | collective-permute-done | bytes 266272 | tf_op jit(solution)/shard_map/ppermute | solution.py:48
  10.4 2.9 %collective-permute-done = bf16[1040,128]{1,0:T(8,128)(2,1)S(1)} collective-permute-done((bf16[1040,128]{1,0:T(8,128)(2,1)S(1)}, bf16[1040,128]{1,0:T(8,128)(2,1)S(1)}, u32[]{:S(2)}, u32[]{:S(2)}) %collective-permute-start) | collective-permute-done | bytes 266272 | tf_op jit(solution)/shard_map/ppermute | solution.py:48
  13.3 0.2 collective-permute-done.2
  13.5 0.1 pad_maximum_fusion.after.refs_2_
  13.6 0.0 copy-start
  13.6 3.1 %collective-permute-start.4 = (bf16[4,1040,128]{2,1,0:T(8,128)(2,1)S(1)}, bf16[4,1040,128]{2,1,0:T(8,128)(2,1)S(1)}, u32[]{:S(2)}, u32[]{:S(2)}) collective-permute-start(bf16[4,1040,128]{2,1,0:T(8,128)(2,1)S(1)} %pad_maximum_fusion.after.refs_2_), channel_id=1, source_target_pairs={{0,96},{1,7},{2,98},{3,1},{4,100},{5,3},{6,102},{7,5},{8,104},{9,1... | collective-permute-start | bytes 3194888 | tf_op jit(solution)/shard_map/ppermute | solution.py:48
  16.7 0.6 collective-permute-start.3
  17.3 0.6 pad_add_fusion.here.refs_0_.refs_1_
  17.9 0.0 copy-done
  17.9 1.6 %shard_map.86 = s32[64,128]{1,0:T(8,128)} custom-call(s32[4]{0:T(128)} %pad_add_fusion.here.refs_0_.refs_1_, bf16[4,1040,128]{2,1,0:T(8,128)(2,1)} %copy-done, s32[1,128]{1,0:T(1,128)} %send_count.1, s32[4,128]{1,0:T(4,128)} %bitcast.46, s32[16,128]{1,0:T(8,128)} %bitcast.45), custom_call_target="tpu_custom_call" | custom-call | bytes 3500000 | tf_op jit(solution)/shard_map/pallas_call | solution.py:365
  19.5 11.1 %all-to-all-start = ((s32[64,1,128]{2,1,0:T(1,128)}), s32[64,1,128]{2,1,0:T(1,128)S(1)}, u32[]{:S(2)}, u32[]{:S(2)}) async-start(s32[64,1,128]{2,1,0:T(1,128)} %bitcast.43), calls=%async_computation | async-start | bytes 65536 | tf_op jit(solution)/shard_map/all_to_all | solution.py:427
  30.7 1.6 %collective-permute-start.6 = (bf16[4,1040,128]{2,1,0:T(8,128)(2,1)}, bf16[4,1040,128]{2,1,0:T(8,128)(2,1)}, u32[]{:S(2)}, u32[]{:S(2)}) collective-permute-start(bf16[4,1040,128]{2,1,0:T(8,128)(2,1)} %copy-done), channel_id=1, source_target_pairs={{0,32},{1,3},{2,34},{3,5},{4,36},{5,7},{6,38},{7,1},{8,40},{9,11},... | collective-permute-start | bytes 3194888 | tf_op jit(solution)/shard_map/ppermute | solution.py:48
  32.3 11.5 %all-to-all-done = s32[64,1,128]{2,1,0:T(1,128)S(1)} async-done(((s32[64,1,128]{2,1,0:T(1,128)}), s32[64,1,128]{2,1,0:T(1,128)S(1)}, u32[]{:S(2)}, u32[]{:S(2)}) %all-to-all-start) | async-done | bytes 32800 | tf_op jit(solution)/shard_map/all_to_all | solution.py:427
  43.9 0.0 collective-permute-done.4.refs_3_
  43.9 0.0 collective-permute-done.3.refs_2_
  43.9 0.0 copy-done.7
  43.9 0.0 copy-start.13
  43.9 0.0 copy-start.1
  43.9 3.4 %shard_map.87 = (bf16[64,64,128]{2,1,0:T(8,128)(2,1)S(1)}, bf16[64,64,128]{2,1,0:T(8,128)(2,1)S(1)}, bf16[64,64,128]{2,1,0:T(8,128)(2,1)}, bf16[64,64,128]{2,1,0:T(8,128)(2,1)S(1)}) custom-call(s32[4]{0:T(128)S(1)} %copy-done.7, s32[64,128]{1,0:T(8,128)S(1)} %bitcast.36, bf16[4,1040,128]{2,1,0:T(8,128)(2,1)S(1)} %collective-permute-done.3.refs_2_, ...), custom_call_target="tpu_custom_call" | custom-call | bytes 14000000 | tf_op jit(solution)/shard_map/pallas_call | solution.py:102
  47.3 0.0 copy-start.2
  47.3 1.0 copy-done.2
  48.3 0.9 collective-permute-start.11
  49.2 2.4 %collective-permute-start.13 = (bf16[64,64,128]{2,1,0:T(8,128)(2,1)S(1)}, bf16[64,64,128]{2,1,0:T(8,128)(2,1)S(1)}, u32[]{:S(2)}, u32[]{:S(2)}) collective-permute-start(bf16[64,64,128]{2,1,0:T(8,128)(2,1)S(1)} %get-tuple-element.23), channel_id=1, source_target_pairs={{0,6},{1,25},{2,0},{3,27},{4,2},{5,29},{6,4},{7,31},{8,14},{9,1},{... | collective-permute-start | bytes 3145736 | tf_op jit(solution)/shard_map/ppermute | solution.py:48
  51.5 0.0 copy-done.13
  51.5 0.0 collective-permute-start.5
  51.6 0.0 collective-permute-done.6.refs_3_
  51.6 0.0 copy-done.1
  51.6 4.5 %shard_map.89 = (bf16[64,64,128]{2,1,0:T(8,128)(2,1)S(1)}, bf16[64,64,128]{2,1,0:T(8,128)(2,1)}, bf16[64,64,128]{2,1,0:T(8,128)(2,1)}, bf16[64,64,128]{2,1,0:T(8,128)(2,1)S(1)}) custom-call(s32[4]{0:T(128)S(1)} %copy-done.7, s32[4]{0:T(128)S(1)} %copy-done.7, bf16[4,1040,128]{2,1,0:T(8,128)(2,1)S(1)} %copy-done.1, ...), custom_call_target="tpu_custom_call" | custom-call | bytes 14000000 | tf_op jit(solution)/shard_map/pallas_call | solution.py:102
  56.1 0.0 copy-start.3
  56.1 1.0 copy-done.3
  57.1 0.0 collective-permute-start.10
  57.1 0.0 collective-permute-done.5
  57.1 3.2 %collective-permute-start.12 = (bf16[64,64,128]{2,1,0:T(8,128)(2,1)S(1)}, bf16[64,64,128]{2,1,0:T(8,128)(2,1)}, u32[]{:S(2)}, u32[]{:S(2)}) collective-permute-start(bf16[64,64,128]{2,1,0:T(8,128)(2,1)S(1)} %get-tuple-element.22), channel_id=1, source_target_pairs={{0,6},{1,25},{2,0},{3,27},{4,2},{5,29},{6,4},{7,31},{8,14},{9,1},{... | collective-permute-start | bytes 3145736 | tf_op jit(solution)/shard_map/ppermute | solution.py:48
  60.4 18.0 %shard_map.88 = (s32[40,128]{1,0:T(8,128)S(1)}, bf16[64,64,128]{2,1,0:T(8,128)(2,1)}) custom-call(s32[4]{0:T(128)S(1)} %copy-done.7, s32[64,128]{1,0:T(8,128)S(1)} %bitcast.37, bf16[64,64,128]{2,1,0:T(8,128)(2,1)} %get-tuple-element.14.held), custom_call_target="tpu_custom_call", output_to_operand_aliasing={{1}: (2, {})} | custom-call | bytes 28000000 | tf_op jit(solution)/shard_map/pallas_call | solution.py:218
  78.3 0.0 copy-start.5
  78.3 0.6 copy-done.5
  78.9 0.0 collective-permute-done.11.refs_6_
  78.9 1.0 copy-done.11
  79.9 0.0 collective-permute-start.8
  79.9 0.0 collective-permute-done.13.refs_8_
  79.9 1.0 copy-done.12
  80.9 3.5 %collective-permute-start.7 = (bf16[64,64,128]{2,1,0:T(8,128)(2,1)}, bf16[64,64,128]{2,1,0:T(8,128)(2,1)}, u32[]{:S(2)}, u32[]{:S(2)}) collective-permute-start(bf16[64,64,128]{2,1,0:T(8,128)(2,1)} %get-tuple-element.16), channel_id=1, source_target_pairs={{0,4},{1,17},{2,6},{3,19},{4,0},{5,21},{6,2},{7,23},{8,12},{9,25},... | collective-permute-start | bytes 3145736 | tf_op jit(solution)/shard_map/ppermute | solution.py:48
  84.5 0.0 collective-permute-done.10.refs_5_
  84.5 0.0 collective-permute-done.12.refs_7_
  84.5 0.0 collective-permute-done.9.refs_10_.refs_6_
  84.5 0.0 slice-start
  84.5 0.5 copy-done.9
  85.0 17.4 %shard_map.90.refs_7_ = f32[64,32]{1,0:T(8,128)} custom-call(s32[4]{0:T(128)} %pad_add_fusion.here.refs_0_.refs_1_, s32[40,128]{1,0:T(8,128)} %copy-done.5, s32[256]{0:T(256)} %copy-done.9, bf16[64,64,128]{2,1,0:T(8,128)(2,1)} %copy-done.3, bf16[64,64,128]{2,1,0:T(8,128)(2,1)} %copy-done.2, bf16[64,64,128]{2,1,0:T(8,128)(2,1)} %collective-permute-done.10.refs_5_, ...), custom_call_target="tpu_custom_call" | custom-call | bytes 42000000 | tf_op jit(solution)/shard_map/pallas_call | solution.py:322
  102.5 0.0 collective-permute-done.8.refs_4_
  102.5 5.3 %collective-permute-done.7.refs_3_ = bf16[64,64,128]{2,1,0:T(8,128)(2,1)} collective-permute-done((bf16[64,64,128]{2,1,0:T(8,128)(2,1)}, bf16[64,64,128]{2,1,0:T(8,128)(2,1)}, u32[]{:S(2)}, u32[]{:S(2)}) %collective-permute-start.7) | collective-permute-done | bytes 1048608 | tf_op jit(solution)/shard_map/ppermute | solution.py:48
  107.8 0.0 slice-done
  107.8 0.0 slice-done.1
  107.8 0.0 copy-done.6
  107.8 0.7 copy-done.4
  108.6 0.7 copy-done.10
  109.2 7.2 %shard_map.91 = f32[64,32]{1,0:T(8,128)S(1)} custom-call(s32[4]{0:T(128)S(1)} %copy-done.8, s32[40,128]{1,0:T(8,128)S(1)} %copy-done.6, s32[256]{0:T(256)S(1)} %copy-done.10, bf16[64,64,128]{2,1,0:T(8,128)(2,1)} %collective-permute-done.7.refs_3_, bf16[64,64,128]{2,1,0:T(8,128)(2,1)S(1)} %collective-permute-done.8.refs_4_, ...), custom_call_target="tpu_custom_call" | custom-call | bytes 28000000 | tf_op jit(solution)/shard_map/pallas_call | solution.py:322
  116.4 20.8 %all_to_all.22 = f32[64,1,32]{2,1,0:T(1,128)} all-to-all(f32[64,1,32]{2,1,0:T(1,128)S(1)} %bitcast.38), channel_id=1, replica_groups=mesh['y'=4,'x'=4,'z'=4,'core'=2] {'y','x','z'}, dimensions={0} | all-to-all | bytes 16384 | tf_op jit(solution)/shard_map/all_to_all | solution.py:444
  137.3 1.8 %shard_map.92 = (f32[16,128]{1,0:T(8,128)}, f32[1,16]{1,0:T(1,128)}) custom-call(s32[4]{0:T(128)} %pad_add_fusion.here.refs_0_.refs_1_, f32[64,32]{1,0:T(8,128)} %bitcast.44, s32[1,128]{1,0:T(1,128)} %send_count.1, s32[4,128]{1,0:T(4,128)} %bitcast.47, s32[4,128]{1,0:T(4,128)} %bitcast.48), custom_call_target="tpu_custom_call" | custom-call | bytes 7000000 | tf_op jit(solution)/shard_map/pallas_call | solution.py:404
  (14 shorter events, 0.1 us)
Async XLA Ops:
  0.6 83.9 %collective-permute-start.9 = (bf16[128,192,128]{2,1,0:T(8,128)(2,1)}, bf16[128,192,128]{2,1,0:T(8,128)(2,1)}, u32[]{:S(2)}, u32[]{:S(2)}) collective-permute-start(bf16[128,192,128]{2,1,0:T(8,128)(2,1)} %refs_5_.1), channel_id=1, source_target_pairs={{0,1},{1,0},{2,3},{3,2},{4,5},{5,4},{6,7},{7,6},{8,9},{9,8},{10,11... | collective-permute-start | bytes 18874376 | tf_op jit(solution)/shard_map/ppermute | solution.py:430
  2.4 8.0 %collective-permute-start.1 = (bf16[1040,128]{1,0:T(8,128)(2,1)S(1)}, bf16[1040,128]{1,0:T(8,128)(2,1)S(1)}, u32[]{:S(2)}, u32[]{:S(2)}) collective-permute-start(bf16[1040,128]{1,0:T(8,128)(2,1)S(1)} %get-tuple-element.27), channel_id=1, source_target_pairs={{0,16},{1,65},{2,18},{3,67},{4,20},{5,69},{6,22},{7,71},{8,24},{9,... | collective-permute-start | bytes 798728 | tf_op jit(solution)/shard_map/ppermute | solution.py:48
  5.6 7.7 %collective-permute-start = (bf16[1040,128]{1,0:T(8,128)(2,1)S(1)}, bf16[1040,128]{1,0:T(8,128)(2,1)S(1)}, u32[]{:S(2)}, u32[]{:S(2)}) collective-permute-start(bf16[1040,128]{1,0:T(8,128)(2,1)S(1)} %get-tuple-element.27), channel_id=1, source_target_pairs={{0,8},{1,33},{2,10},{3,35},{4,12},{5,37},{6,14},{7,39},{8,16},{9,4... | collective-permute-start | bytes 798728 | tf_op jit(solution)/shard_map/ppermute | solution.py:48
  6.2 7.2 %collective-permute-start.2 = (bf16[1040,128]{1,0:T(8,128)(2,1)S(1)}, bf16[1040,128]{1,0:T(8,128)(2,1)S(1)}, u32[]{:S(2)}, u32[]{:S(2)}) collective-permute-start(bf16[1040,128]{1,0:T(8,128)(2,1)S(1)} %get-tuple-element.27), channel_id=1, source_target_pairs={{0,24},{1,97},{2,26},{3,99},{4,28},{5,101},{6,30},{7,103},{8,0},{9... | collective-permute-start | bytes 798728 | tf_op jit(solution)/shard_map/ppermute | solution.py:48
  13.6 4.3 %copy-start = (bf16[4,1040,128]{2,1,0:T(8,128)(2,1)}, bf16[4,1040,128]{2,1,0:T(8,128)(2,1)S(1)}, u32[]{:S(2)}) copy-start(bf16[4,1040,128]{2,1,0:T(8,128)(2,1)S(1)} %pad_maximum_fusion.after.refs_2_) | copy-start | bytes 3194884
  13.6 30.3 %collective-permute-start.4 = (bf16[4,1040,128]{2,1,0:T(8,128)(2,1)S(1)}, bf16[4,1040,128]{2,1,0:T(8,128)(2,1)S(1)}, u32[]{:S(2)}, u32[]{:S(2)}) collective-permute-start(bf16[4,1040,128]{2,1,0:T(8,128)(2,1)S(1)} %pad_maximum_fusion.after.refs_2_), channel_id=1, source_target_pairs={{0,96},{1,7},{2,98},{3,1},{4,100},{5,3},{6,102},{7,5},{8,104},{9,1... | collective-permute-start | bytes 3194888 | tf_op jit(solution)/shard_map/ppermute | solution.py:48
  16.7 27.2 %collective-permute-start.3 = (bf16[4,1040,128]{2,1,0:T(8,128)(2,1)S(1)}, bf16[4,1040,128]{2,1,0:T(8,128)(2,1)S(1)}, u32[]{:S(2)}, u32[]{:S(2)}) collective-permute-start(bf16[4,1040,128]{2,1,0:T(8,128)(2,1)S(1)} %pad_maximum_fusion.after.refs_2_), channel_id=1, source_target_pairs={{0,64},{1,5},{2,66},{3,7},{4,68},{5,1},{6,70},{7,3},{8,72},{9,13},... | collective-permute-start | bytes 3194888 | tf_op jit(solution)/shard_map/ppermute | solution.py:48
  17.9 25.9 %copy-start.7 = (s32[4]{0:T(128)S(1)}, s32[4]{0:T(128)}, u32[]{:S(2)}) copy-start(s32[4]{0:T(128)} %pad_add_fusion.here.refs_0_.refs_1_) | copy-start | bytes 52
  19.5 24.3 %all-to-all-start = ((s32[64,1,128]{2,1,0:T(1,128)}), s32[64,1,128]{2,1,0:T(1,128)S(1)}, u32[]{:S(2)}, u32[]{:S(2)}) async-start(s32[64,1,128]{2,1,0:T(1,128)} %bitcast.43), calls=%async_computation | async-start | bytes 65536 | tf_op jit(solution)/shard_map/all_to_all | solution.py:427
  30.7 20.9 %collective-permute-start.6 = (bf16[4,1040,128]{2,1,0:T(8,128)(2,1)}, bf16[4,1040,128]{2,1,0:T(8,128)(2,1)}, u32[]{:S(2)}, u32[]{:S(2)}) collective-permute-start(bf16[4,1040,128]{2,1,0:T(8,128)(2,1)} %copy-done), channel_id=1, source_target_pairs={{0,32},{1,3},{2,34},{3,5},{4,36},{5,7},{6,38},{7,1},{8,40},{9,11},... | collective-permute-start | bytes 3194888 | tf_op jit(solution)/shard_map/ppermute | solution.py:48
  43.9 7.7 %copy-start.13 = (s32[128]{0:T(128)S(1)}, s32[128]{0:T(128)}, u32[]{:S(2)}) copy-start(s32[128]{0:T(128)} %param.9) | copy-start | bytes 1540
  43.9 7.7 %copy-start.1 = (bf16[4,1040,128]{2,1,0:T(8,128)(2,1)S(1)}, bf16[4,1040,128]{2,1,0:T(8,128)(2,1)}, u32[]{:S(2)}) copy-start(bf16[4,1040,128]{2,1,0:T(8,128)(2,1)} %copy-done) | copy-start | bytes 3194884
  47.3 1.0 copy-start.2
  48.3 30.6 %collective-permute-start.11 = (bf16[64,64,128]{2,1,0:T(8,128)(2,1)S(1)}, bf16[64,64,128]{2,1,0:T(8,128)(2,1)S(1)}, u32[]{:S(2)}, u32[]{:S(2)}) collective-permute-start(bf16[64,64,128]{2,1,0:T(8,128)(2,1)S(1)} %get-tuple-element.21), channel_id=1, source_target_pairs={{0,2},{1,9},{2,4},{3,11},{4,6},{5,13},{6,0},{7,15},{8,10},{9,17},{... | collective-permute-start | bytes 3145736 | tf_op jit(solution)/shard_map/ppermute | solution.py:48
  49.2 30.8 %collective-permute-start.13 = (bf16[64,64,128]{2,1,0:T(8,128)(2,1)S(1)}, bf16[64,64,128]{2,1,0:T(8,128)(2,1)S(1)}, u32[]{:S(2)}, u32[]{:S(2)}) collective-permute-start(bf16[64,64,128]{2,1,0:T(8,128)(2,1)S(1)} %get-tuple-element.23), channel_id=1, source_target_pairs={{0,6},{1,25},{2,0},{3,27},{4,2},{5,29},{6,4},{7,31},{8,14},{9,1},{... | collective-permute-start | bytes 3145736 | tf_op jit(solution)/shard_map/ppermute | solution.py:48
  51.5 5.6 %collective-permute-start.5 = (s32[128]{0:T(128)S(1)}, s32[128]{0:T(128)S(1)}, u32[]{:S(2)}, u32[]{:S(2)}) collective-permute-start(s32[128]{0:T(128)S(1)} %copy-done.13), channel_id=1, source_target_pairs={{0,1},{1,0},{2,3},{3,2},{4,5},{5,4},{6,7},{7,6},{8,9},{9,8},{10,11... | collective-permute-start | bytes 1544 | tf_op jit(solution)/shard_map/ppermute | solution.py:431
  56.1 1.0 copy-start.3
  57.1 27.3 %collective-permute-start.10 = (bf16[64,64,128]{2,1,0:T(8,128)(2,1)}, bf16[64,64,128]{2,1,0:T(8,128)(2,1)}, u32[]{:S(2)}, u32[]{:S(2)}) collective-permute-start(bf16[64,64,128]{2,1,0:T(8,128)(2,1)} %get-tuple-element.20), channel_id=1, source_target_pairs={{0,2},{1,9},{2,4},{3,11},{4,6},{5,13},{6,0},{7,15},{8,10},{9,17},{... | collective-permute-start | bytes 3145736 | tf_op jit(solution)/shard_map/ppermute | solution.py:48
  57.1 27.3 %collective-permute-start.12 = (bf16[64,64,128]{2,1,0:T(8,128)(2,1)S(1)}, bf16[64,64,128]{2,1,0:T(8,128)(2,1)}, u32[]{:S(2)}, u32[]{:S(2)}) collective-permute-start(bf16[64,64,128]{2,1,0:T(8,128)(2,1)S(1)} %get-tuple-element.22), channel_id=1, source_target_pairs={{0,6},{1,25},{2,0},{3,27},{4,2},{5,29},{6,4},{7,31},{8,14},{9,1},{... | collective-permute-start | bytes 3145736 | tf_op jit(solution)/shard_map/ppermute | solution.py:48
  78.3 0.6 copy-start.5
  78.9 1.0 copy-start.11
  79.9 22.5 %collective-permute-start.8 = (bf16[64,64,128]{2,1,0:T(8,128)(2,1)}, bf16[64,64,128]{2,1,0:T(8,128)(2,1)S(1)}, u32[]{:S(2)}, u32[]{:S(2)}) collective-permute-start(bf16[64,64,128]{2,1,0:T(8,128)(2,1)} %get-tuple-element.17), channel_id=1, source_target_pairs={{0,4},{1,17},{2,6},{3,19},{4,0},{5,21},{6,2},{7,23},{8,12},{9,25},... | collective-permute-start | bytes 3145736 | tf_op jit(solution)/shard_map/ppermute | solution.py:48
  79.9 1.0 copy-start.12
  80.9 26.9 %collective-permute-start.7 = (bf16[64,64,128]{2,1,0:T(8,128)(2,1)}, bf16[64,64,128]{2,1,0:T(8,128)(2,1)}, u32[]{:S(2)}, u32[]{:S(2)}) collective-permute-start(bf16[64,64,128]{2,1,0:T(8,128)(2,1)} %get-tuple-element.16), channel_id=1, source_target_pairs={{0,4},{1,17},{2,6},{3,19},{4,0},{5,21},{6,2},{7,23},{8,12},{9,25},... | collective-permute-start | bytes 3145736 | tf_op jit(solution)/shard_map/ppermute | solution.py:48
  84.5 0.6 copy-start.9
  84.5 23.3 %slice-start = ((s8[6291456]{0:T(1024)(128)(4,1)}), s8[4194304]{0:T(1024)(128)(4,1)S(1)}, s32[]{:S(2)}) async-start(s8[6291456]{0:T(1024)(128)(4,1)} %bitcast.34), calls=%async_computation.2 | async-start | bytes 8388608
  85.0 22.8 %slice-start.1 = ((s8[6291456]{0:T(1024)(128)(4,1)}), s8[2097152]{0:T(1024)(128)(4,1)S(1)}, s32[]{:S(2)}) async-start(s8[6291456]{0:T(1024)(128)(4,1)} %bitcast.34), calls=%async_computation.3 | async-start | bytes 4194304
  85.0 22.8 %copy-start.6 = (s32[40,128]{1,0:T(8,128)S(1)}, s32[40,128]{1,0:T(8,128)}, u32[]{:S(2)}) copy-start(s32[40,128]{1,0:T(8,128)} %copy-done.5) | copy-start | bytes 61444
  85.0 22.8 %copy-start.8 = (s32[4]{0:T(128)S(1)}, s32[4]{0:T(128)}, u32[]{:S(2)}) copy-start(s32[4]{0:T(128)} %pad_add_fusion.here.refs_0_.refs_1_) | copy-start | bytes 52
  107.8 0.8 copy-start.4
  108.6 0.7 copy-start.10

commit v4 on v3

--- a/solution.py
+++ b/solution.py
@@ -15,7 +15,7 @@
 CAPS = 4
 SLOTS = 4
 LANE = 4
-UNROLL = 16
+UNROLL = 32
 NOBODY = EARLY * 2 * SLOTS * CAPS
 MIB = 1 << 20
 CONTS = 16

time: 139 us -> 138 us (level)
  Pallas kernels: 53.9 us -> 49 us
  waiting for transfers between devices: 21.5 us -> 25.6 us
    pallas_call x2, Pallas kernels: 24.6 us -> 19.7 us  [score(): pl.pallas_call(lambda *refs: score_kernel(part, many, *refs), out_shape=j...]
    ppermute x12, waiting for transfers between devices: 9.92 us -> 14.1 us  [shift(): return lax.ppermute(array, ALL, pairs)]
  transfers between devices with their start and end apart: 15 -> 15, of which waited for: 5 -> 5; matrix products, arithmetic and copies ran while one was open for 2% -> 2% of each run, Pallas kernels for 32% -> 30%
where the time goes in v4:
time: 138 us; the launch traced here: 137 us
  Pallas kernels  49 us (36%)
  starting transfers between devices  33 us (24%)
  waiting for transfers between devices  25.6 us (19%)
  blocking collectives  19.9 us (14%)
  local copies, waits for them, and re-layouts  6.57 us (5%)
  other arithmetic  2.46 us (2%)
    ppermute x12, starting transfers between devices, shift(): return lax.ppermute(array, ALL, pairs)  21.8 us
    all_to_all x1, blocking collectives, body(): lax.all_to_all(handled, PLACE, split_axis=0, concat_axis=0, tiled=True)  19.9 us
    pallas_call x2, Pallas kernels, score(): pl.pallas_call(lambda *refs: score_kernel(part, many, *refs), out_shape=j...  19.7 us
    pallas_call x1, Pallas kernels, group_pairs(): pl.pallas_call(group_kernel, out_shape=(jax.ShapeDtypeStruct((rows, 128),...  18 us
    ppermute x12, waiting for transfers between devices, shift(): return lax.ppermute(array, ALL, pairs)  14.1 us
    all_to_all x1, waiting for transfers between devices, body(): lax.all_to_all(notes, PLACE, split_axis=0, concat_axis=0, tiled=True)  11.5 us
    all_to_all x1, starting transfers between devices, body(): lax.all_to_all(notes, PLACE, split_axis=0, concat_axis=0, tiled=True)  11.1 us
    pallas_call x2, Pallas kernels, select(): pl.pallas_call(lambda *refs: select_kernel(targets, *refs), out_shape=[ja...  7.94 us
  transfers between devices with their start and end apart: 15, of which 5 were waited for; matrix products, arithmetic and copies ran while one was open for 2% of the time, Pallas kernels for 30%

profile of v4, /device:TPU:0, one launch (start us, length us, event | category | flops | bytes accessed | tf_op | source)
XLA Modules:
  0.0 137.3 jit_solution(15766388981012431408)
XLA Ops:
  0.6 0.1 collective-permute-start.9
  0.7 0.7 bitcast_convert_fusion
  1.4 1.0 fusion.2
  2.4 3.2 %collective-permute-start.1 = (bf16[1040,128]{1,0:T(8,128)(2,1)S(1)}, bf16[1040,128]{1,0:T(8,128)(2,1)S(1)}, u32[]{:S(2)}, u32[]{:S(2)}) collective-permute-start(bf16[1040,128]{1,0:T(8,128)(2,1)S(1)} %get-tuple-element.27), channel_id=1, source_target_pairs={{0,16},{1,65},{2,18},{3,67},{4,20},{5,69},{6,22},{7,71},{8,24},{9,... | collective-permute-start | bytes 798728 | tf_op jit(solution)/shard_map/ppermute | solution.py:48
  5.6 0.6 collective-permute-start
  6.2 2.6 %collective-permute-start.2 = (bf16[1040,128]{1,0:T(8,128)(2,1)S(1)}, bf16[1040,128]{1,0:T(8,128)(2,1)S(1)}, u32[]{:S(2)}, u32[]{:S(2)}) collective-permute-start(bf16[1040,128]{1,0:T(8,128)(2,1)S(1)} %get-tuple-element.27), channel_id=1, source_target_pairs={{0,24},{1,97},{2,26},{3,99},{4,28},{5,101},{6,30},{7,103},{8,0},{9... | collective-permute-start | bytes 798728 | tf_op jit(solution)/shard_map/ppermute | solution.py:48
  8.9 1.6 %collective-permute-done.1 = bf16[1040,128]{1,0:T(8,128)(2,1)S(1)} collective-permute-done((bf16[1040,128]{1,0:T(8,128)(2,1)S(1)}, bf16[1040,128]{1,0:T(8,128)(2,1)S(1)}, u32[]{:S(2)}, u32[]{:S(2)}) %collective-permute-start.1) | collective-permute-done | bytes 266272 | tf_op jit(solution)/shard_map/ppermute | solution.py:48
  10.4 2.9 %collective-permute-done = bf16[1040,128]{1,0:T(8,128)(2,1)S(1)} collective-permute-done((bf16[1040,128]{1,0:T(8,128)(2,1)S(1)}, bf16[1040,128]{1,0:T(8,128)(2,1)S(1)}, u32[]{:S(2)}, u32[]{:S(2)}) %collective-permute-start) | collective-permute-done | bytes 266272 | tf_op jit(solution)/shard_map/ppermute | solution.py:48
  13.3 0.2 collective-permute-done.2
  13.5 0.1 pad_maximum_fusion.after.refs_2_
  13.6 0.0 copy-start
  13.6 3.1 %collective-permute-start.4 = (bf16[4,1040,128]{2,1,0:T(8,128)(2,1)S(1)}, bf16[4,1040,128]{2,1,0:T(8,128)(2,1)S(1)}, u32[]{:S(2)}, u32[]{:S(2)}) collective-permute-start(bf16[4,1040,128]{2,1,0:T(8,128)(2,1)S(1)} %pad_maximum_fusion.after.refs_2_), channel_id=1, source_target_pairs={{0,96},{1,7},{2,98},{3,1},{4,100},{5,3},{6,102},{7,5},{8,104},{9,1... | collective-permute-start | bytes 3194888 | tf_op jit(solution)/shard_map/ppermute | solution.py:48
  16.7 0.6 collective-permute-start.3
  17.3 0.6 pad_add_fusion.here.refs_0_.refs_1_
  17.9 0.0 copy-done
  17.9 1.6 %shard_map.86 = s32[64,128]{1,0:T(8,128)} custom-call(s32[4]{0:T(128)} %pad_add_fusion.here.refs_0_.refs_1_, bf16[4,1040,128]{2,1,0:T(8,128)(2,1)} %copy-done, s32[1,128]{1,0:T(1,128)} %send_count.1, s32[4,128]{1,0:T(4,128)} %bitcast.46, s32[16,128]{1,0:T(8,128)} %bitcast.45), custom_call_target="tpu_custom_call" | custom-call | bytes 3500000 | tf_op jit(solution)/shard_map/pallas_call | solution.py:365
  19.5 11.1 %all-to-all-start = ((s32[64,1,128]{2,1,0:T(1,128)}), s32[64,1,128]{2,1,0:T(1,128)S(1)}, u32[]{:S(2)}, u32[]{:S(2)}) async-start(s32[64,1,128]{2,1,0:T(1,128)} %bitcast.43), calls=%async_computation | async-start | bytes 65536 | tf_op jit(solution)/shard_map/all_to_all | solution.py:427
  30.7 1.6 %collective-permute-start.6 = (bf16[4,1040,128]{2,1,0:T(8,128)(2,1)}, bf16[4,1040,128]{2,1,0:T(8,128)(2,1)}, u32[]{:S(2)}, u32[]{:S(2)}) collective-permute-start(bf16[4,1040,128]{2,1,0:T(8,128)(2,1)} %copy-done), channel_id=1, source_target_pairs={{0,32},{1,3},{2,34},{3,5},{4,36},{5,7},{6,38},{7,1},{8,40},{9,11},... | collective-permute-start | bytes 3194888 | tf_op jit(solution)/shard_map/ppermute | solution.py:48
  32.3 11.5 %all-to-all-done = s32[64,1,128]{2,1,0:T(1,128)S(1)} async-done(((s32[64,1,128]{2,1,0:T(1,128)}), s32[64,1,128]{2,1,0:T(1,128)S(1)}, u32[]{:S(2)}, u32[]{:S(2)}) %all-to-all-start) | async-done | bytes 32800 | tf_op jit(solution)/shard_map/all_to_all | solution.py:427
  43.9 0.0 collective-permute-done.4.refs_3_
  43.9 0.0 collective-permute-done.3.refs_2_
  43.9 0.0 copy-done.7
  43.9 0.0 copy-start.13
  43.9 0.0 copy-start.1
  43.9 3.4 %shard_map.87 = (bf16[64,64,128]{2,1,0:T(8,128)(2,1)S(1)}, bf16[64,64,128]{2,1,0:T(8,128)(2,1)S(1)}, bf16[64,64,128]{2,1,0:T(8,128)(2,1)}, bf16[64,64,128]{2,1,0:T(8,128)(2,1)S(1)}) custom-call(s32[4]{0:T(128)S(1)} %copy-done.7, s32[64,128]{1,0:T(8,128)S(1)} %bitcast.36, bf16[4,1040,128]{2,1,0:T(8,128)(2,1)S(1)} %collective-permute-done.3.refs_2_, ...), custom_call_target="tpu_custom_call" | custom-call | bytes 14000000 | tf_op jit(solution)/shard_map/pallas_call | solution.py:102
  47.3 0.0 copy-start.2
  47.3 1.0 copy-done.2
  48.3 0.9 collective-permute-start.11
  49.2 2.4 %collective-permute-start.13 = (bf16[64,64,128]{2,1,0:T(8,128)(2,1)S(1)}, bf16[64,64,128]{2,1,0:T(8,128)(2,1)S(1)}, u32[]{:S(2)}, u32[]{:S(2)}) collective-permute-start(bf16[64,64,128]{2,1,0:T(8,128)(2,1)S(1)} %get-tuple-element.23), channel_id=1, source_target_pairs={{0,6},{1,25},{2,0},{3,27},{4,2},{5,29},{6,4},{7,31},{8,14},{9,1},{... | collective-permute-start | bytes 3145736 | tf_op jit(solution)/shard_map/ppermute | solution.py:48
  51.5 0.0 copy-done.13
  51.5 0.0 collective-permute-start.5
  51.6 0.0 collective-permute-done.6.refs_3_
  51.6 0.0 copy-done.1
  51.6 4.5 %shard_map.89 = (bf16[64,64,128]{2,1,0:T(8,128)(2,1)S(1)}, bf16[64,64,128]{2,1,0:T(8,128)(2,1)}, bf16[64,64,128]{2,1,0:T(8,128)(2,1)}, bf16[64,64,128]{2,1,0:T(8,128)(2,1)S(1)}) custom-call(s32[4]{0:T(128)S(1)} %copy-done.7, s32[4]{0:T(128)S(1)} %copy-done.7, bf16[4,1040,128]{2,1,0:T(8,128)(2,1)S(1)} %copy-done.1, ...), custom_call_target="tpu_custom_call" | custom-call | bytes 14000000 | tf_op jit(solution)/shard_map/pallas_call | solution.py:102
  56.1 0.0 copy-start.3
  56.1 1.0 copy-done.3
  57.1 0.0 collective-permute-start.10
  57.1 0.0 collective-permute-done.5
  57.1 3.2 %collective-permute-start.12 = (bf16[64,64,128]{2,1,0:T(8,128)(2,1)S(1)}, bf16[64,64,128]{2,1,0:T(8,128)(2,1)}, u32[]{:S(2)}, u32[]{:S(2)}) collective-permute-start(bf16[64,64,128]{2,1,0:T(8,128)(2,1)S(1)} %get-tuple-element.22), channel_id=1, source_target_pairs={{0,6},{1,25},{2,0},{3,27},{4,2},{5,29},{6,4},{7,31},{8,14},{9,1},{... | collective-permute-start | bytes 3145736 | tf_op jit(solution)/shard_map/ppermute | solution.py:48
  60.4 18.0 %shard_map.88 = (s32[40,128]{1,0:T(8,128)S(1)}, bf16[64,64,128]{2,1,0:T(8,128)(2,1)}) custom-call(s32[4]{0:T(128)S(1)} %copy-done.7, s32[64,128]{1,0:T(8,128)S(1)} %bitcast.37, bf16[64,64,128]{2,1,0:T(8,128)(2,1)} %get-tuple-element.14.held), custom_call_target="tpu_custom_call", output_to_operand_aliasing={{1}: (2, {})} | custom-call | bytes 28000000 | tf_op jit(solution)/shard_map/pallas_call | solution.py:218
  78.3 0.0 copy-start.5
  78.3 0.6 copy-done.5
  78.9 0.0 collective-permute-done.11.refs_6_
  78.9 1.0 copy-done.11
  79.9 0.0 collective-permute-start.8
  79.9 0.0 collective-permute-done.13.refs_8_
  79.9 1.0 copy-done.12
  80.9 3.5 %collective-permute-start.7 = (bf16[64,64,128]{2,1,0:T(8,128)(2,1)}, bf16[64,64,128]{2,1,0:T(8,128)(2,1)}, u32[]{:S(2)}, u32[]{:S(2)}) collective-permute-start(bf16[64,64,128]{2,1,0:T(8,128)(2,1)} %get-tuple-element.16), channel_id=1, source_target_pairs={{0,4},{1,17},{2,6},{3,19},{4,0},{5,21},{6,2},{7,23},{8,12},{9,25},... | collective-permute-start | bytes 3145736 | tf_op jit(solution)/shard_map/ppermute | solution.py:48
  84.5 0.0 collective-permute-done.10.refs_5_
  84.5 0.0 collective-permute-done.12.refs_7_
  84.5 0.0 collective-permute-done.9.refs_10_.refs_6_
  84.5 0.0 slice-start
  84.5 0.5 copy-done.9
  85.0 13.3 %shard_map.90.refs_7_ = f32[64,32]{1,0:T(8,128)} custom-call(s32[4]{0:T(128)} %pad_add_fusion.here.refs_0_.refs_1_, s32[40,128]{1,0:T(8,128)} %copy-done.5, s32[256]{0:T(256)} %copy-done.9, bf16[64,64,128]{2,1,0:T(8,128)(2,1)} %copy-done.3, bf16[64,64,128]{2,1,0:T(8,128)(2,1)} %copy-done.2, bf16[64,64,128]{2,1,0:T(8,128)(2,1)} %collective-permute-done.10.refs_5_, ...), custom_call_target="tpu_custom_call" | custom-call | bytes 42000000 | tf_op jit(solution)/shard_map/pallas_call | solution.py:322
  98.3 0.0 collective-permute-done.8.refs_4_
  98.3 9.4 %collective-permute-done.7.refs_3_ = bf16[64,64,128]{2,1,0:T(8,128)(2,1)} collective-permute-done((bf16[64,64,128]{2,1,0:T(8,128)(2,1)}, bf16[64,64,128]{2,1,0:T(8,128)(2,1)}, u32[]{:S(2)}, u32[]{:S(2)}) %collective-permute-start.7) | collective-permute-done | bytes 1048608 | tf_op jit(solution)/shard_map/ppermute | solution.py:48
  107.8 0.0 slice-done
  107.8 0.0 slice-done.1
  107.8 0.0 copy-done.6
  107.8 0.7 copy-done.4
  108.6 0.7 copy-done.10
  109.2 6.4 %shard_map.91 = f32[64,32]{1,0:T(8,128)S(1)} custom-call(s32[4]{0:T(128)S(1)} %copy-done.8, s32[40,128]{1,0:T(8,128)S(1)} %copy-done.6, s32[256]{0:T(256)S(1)} %copy-done.10, bf16[64,64,128]{2,1,0:T(8,128)(2,1)} %collective-permute-done.7.refs_3_, bf16[64,64,128]{2,1,0:T(8,128)(2,1)S(1)} %collective-permute-done.8.refs_4_, ...), custom_call_target="tpu_custom_call" | custom-call | bytes 28000000 | tf_op jit(solution)/shard_map/pallas_call | solution.py:322
  115.7 19.9 %all_to_all.22 = f32[64,1,32]{2,1,0:T(1,128)} all-to-all(f32[64,1,32]{2,1,0:T(1,128)S(1)} %bitcast.38), channel_id=1, replica_groups=mesh['y'=4,'x'=4,'z'=4,'core'=2] {'y','x','z'}, dimensions={0} | all-to-all | bytes 16384 | tf_op jit(solution)/shard_map/all_to_all | solution.py:444
  135.6 1.8 %shard_map.92 = (f32[16,128]{1,0:T(8,128)}, f32[1,16]{1,0:T(1,128)}) custom-call(s32[4]{0:T(128)} %pad_add_fusion.here.refs_0_.refs_1_, f32[64,32]{1,0:T(8,128)} %bitcast.44, s32[1,128]{1,0:T(1,128)} %send_count.1, s32[4,128]{1,0:T(4,128)} %bitcast.47, s32[4,128]{1,0:T(4,128)} %bitcast.48), custom_call_target="tpu_custom_call" | custom-call | bytes 7000000 | tf_op jit(solution)/shard_map/pallas_call | solution.py:404
  (14 shorter events, 0.1 us)
Async XLA Ops:
  0.6 83.9 %collective-permute-start.9 = (bf16[128,192,128]{2,1,0:T(8,128)(2,1)}, bf16[128,192,128]{2,1,0:T(8,128)(2,1)}, u32[]{:S(2)}, u32[]{:S(2)}) collective-permute-start(bf16[128,192,128]{2,1,0:T(8,128)(2,1)} %refs_5_.1), channel_id=1, source_target_pairs={{0,1},{1,0},{2,3},{3,2},{4,5},{5,4},{6,7},{7,6},{8,9},{9,8},{10,11... | collective-permute-start | bytes 18874376 | tf_op jit(solution)/shard_map/ppermute | solution.py:430
  2.4 8.0 %collective-permute-start.1 = (bf16[1040,128]{1,0:T(8,128)(2,1)S(1)}, bf16[1040,128]{1,0:T(8,128)(2,1)S(1)}, u32[]{:S(2)}, u32[]{:S(2)}) collective-permute-start(bf16[1040,128]{1,0:T(8,128)(2,1)S(1)} %get-tuple-element.27), channel_id=1, source_target_pairs={{0,16},{1,65},{2,18},{3,67},{4,20},{5,69},{6,22},{7,71},{8,24},{9,... | collective-permute-start | bytes 798728 | tf_op jit(solution)/shard_map/ppermute | solution.py:48
  5.6 7.7 %collective-permute-start = (bf16[1040,128]{1,0:T(8,128)(2,1)S(1)}, bf16[1040,128]{1,0:T(8,128)(2,1)S(1)}, u32[]{:S(2)}, u32[]{:S(2)}) collective-permute-start(bf16[1040,128]{1,0:T(8,128)(2,1)S(1)} %get-tuple-element.27), channel_id=1, source_target_pairs={{0,8},{1,33},{2,10},{3,35},{4,12},{5,37},{6,14},{7,39},{8,16},{9,4... | collective-permute-start | bytes 798728 | tf_op jit(solution)/shard_map/ppermute | solution.py:48
  6.2 7.2 %collective-permute-start.2 = (bf16[1040,128]{1,0:T(8,128)(2,1)S(1)}, bf16[1040,128]{1,0:T(8,128)(2,1)S(1)}, u32[]{:S(2)}, u32[]{:S(2)}) collective-permute-start(bf16[1040,128]{1,0:T(8,128)(2,1)S(1)} %get-tuple-element.27), channel_id=1, source_target_pairs={{0,24},{1,97},{2,26},{3,99},{4,28},{5,101},{6,30},{7,103},{8,0},{9... | collective-permute-start | bytes 798728 | tf_op jit(solution)/shard_map/ppermute | solution.py:48
  13.6 4.3 %copy-start = (bf16[4,1040,128]{2,1,0:T(8,128)(2,1)}, bf16[4,1040,128]{2,1,0:T(8,128)(2,1)S(1)}, u32[]{:S(2)}) copy-start(bf16[4,1040,128]{2,1,0:T(8,128)(2,1)S(1)} %pad_maximum_fusion.after.refs_2_) | copy-start | bytes 3194884
  13.6 30.3 %collective-permute-start.4 = (bf16[4,1040,128]{2,1,0:T(8,128)(2,1)S(1)}, bf16[4,1040,128]{2,1,0:T(8,128)(2,1)S(1)}, u32[]{:S(2)}, u32[]{:S(2)}) collective-permute-start(bf16[4,1040,128]{2,1,0:T(8,128)(2,1)S(1)} %pad_maximum_fusion.after.refs_2_), channel_id=1, source_target_pairs={{0,96},{1,7},{2,98},{3,1},{4,100},{5,3},{6,102},{7,5},{8,104},{9,1... | collective-permute-start | bytes 3194888 | tf_op jit(solution)/shard_map/ppermute | solution.py:48
  16.7 27.2 %collective-permute-start.3 = (bf16[4,1040,128]{2,1,0:T(8,128)(2,1)S(1)}, bf16[4,1040,128]{2,1,0:T(8,128)(2,1)S(1)}, u32[]{:S(2)}, u32[]{:S(2)}) collective-permute-start(bf16[4,1040,128]{2,1,0:T(8,128)(2,1)S(1)} %pad_maximum_fusion.after.refs_2_), channel_id=1, source_target_pairs={{0,64},{1,5},{2,66},{3,7},{4,68},{5,1},{6,70},{7,3},{8,72},{9,13},... | collective-permute-start | bytes 3194888 | tf_op jit(solution)/shard_map/ppermute | solution.py:48
  17.9 25.9 %copy-start.7 = (s32[4]{0:T(128)S(1)}, s32[4]{0:T(128)}, u32[]{:S(2)}) copy-start(s32[4]{0:T(128)} %pad_add_fusion.here.refs_0_.refs_1_) | copy-start | bytes 52
  19.5 24.3 %all-to-all-start = ((s32[64,1,128]{2,1,0:T(1,128)}), s32[64,1,128]{2,1,0:T(1,128)S(1)}, u32[]{:S(2)}, u32[]{:S(2)}) async-start(s32[64,1,128]{2,1,0:T(1,128)} %bitcast.43), calls=%async_computation | async-start | bytes 65536 | tf_op jit(solution)/shard_map/all_to_all | solution.py:427
  30.7 20.9 %collective-permute-start.6 = (bf16[4,1040,128]{2,1,0:T(8,128)(2,1)}, bf16[4,1040,128]{2,1,0:T(8,128)(2,1)}, u32[]{:S(2)}, u32[]{:S(2)}) collective-permute-start(bf16[4,1040,128]{2,1,0:T(8,128)(2,1)} %copy-done), channel_id=1, source_target_pairs={{0,32},{1,3},{2,34},{3,5},{4,36},{5,7},{6,38},{7,1},{8,40},{9,11},... | collective-permute-start | bytes 3194888 | tf_op jit(solution)/shard_map/ppermute | solution.py:48
  43.9 7.7 %copy-start.13 = (s32[128]{0:T(128)S(1)}, s32[128]{0:T(128)}, u32[]{:S(2)}) copy-start(s32[128]{0:T(128)} %param.9) | copy-start | bytes 1540
  43.9 7.7 %copy-start.1 = (bf16[4,1040,128]{2,1,0:T(8,128)(2,1)S(1)}, bf16[4,1040,128]{2,1,0:T(8,128)(2,1)}, u32[]{:S(2)}) copy-start(bf16[4,1040,128]{2,1,0:T(8,128)(2,1)} %copy-done) | copy-start | bytes 3194884
  47.3 1.0 copy-start.2
  48.3 30.6 %collective-permute-start.11 = (bf16[64,64,128]{2,1,0:T(8,128)(2,1)S(1)}, bf16[64,64,128]{2,1,0:T(8,128)(2,1)S(1)}, u32[]{:S(2)}, u32[]{:S(2)}) collective-permute-start(bf16[64,64,128]{2,1,0:T(8,128)(2,1)S(1)} %get-tuple-element.21), channel_id=1, source_target_pairs={{0,2},{1,9},{2,4},{3,11},{4,6},{5,13},{6,0},{7,15},{8,10},{9,17},{... | collective-permute-start | bytes 3145736 | tf_op jit(solution)/shard_map/ppermute | solution.py:48
  49.2 30.8 %collective-permute-start.13 = (bf16[64,64,128]{2,1,0:T(8,128)(2,1)S(1)}, bf16[64,64,128]{2,1,0:T(8,128)(2,1)S(1)}, u32[]{:S(2)}, u32[]{:S(2)}) collective-permute-start(bf16[64,64,128]{2,1,0:T(8,128)(2,1)S(1)} %get-tuple-element.23), channel_id=1, source_target_pairs={{0,6},{1,25},{2,0},{3,27},{4,2},{5,29},{6,4},{7,31},{8,14},{9,1},{... | collective-permute-start | bytes 3145736 | tf_op jit(solution)/shard_map/ppermute | solution.py:48
  51.5 5.6 %collective-permute-start.5 = (s32[128]{0:T(128)S(1)}, s32[128]{0:T(128)S(1)}, u32[]{:S(2)}, u32[]{:S(2)}) collective-permute-start(s32[128]{0:T(128)S(1)} %copy-done.13), channel_id=1, source_target_pairs={{0,1},{1,0},{2,3},{3,2},{4,5},{5,4},{6,7},{7,6},{8,9},{9,8},{10,11... | collective-permute-start | bytes 1544 | tf_op jit(solution)/shard_map/ppermute | solution.py:431
  56.1 1.0 copy-start.3
  57.1 27.3 %collective-permute-start.10 = (bf16[64,64,128]{2,1,0:T(8,128)(2,1)}, bf16[64,64,128]{2,1,0:T(8,128)(2,1)}, u32[]{:S(2)}, u32[]{:S(2)}) collective-permute-start(bf16[64,64,128]{2,1,0:T(8,128)(2,1)} %get-tuple-element.20), channel_id=1, source_target_pairs={{0,2},{1,9},{2,4},{3,11},{4,6},{5,13},{6,0},{7,15},{8,10},{9,17},{... | collective-permute-start | bytes 3145736 | tf_op jit(solution)/shard_map/ppermute | solution.py:48
  57.1 27.3 %collective-permute-start.12 = (bf16[64,64,128]{2,1,0:T(8,128)(2,1)S(1)}, bf16[64,64,128]{2,1,0:T(8,128)(2,1)}, u32[]{:S(2)}, u32[]{:S(2)}) collective-permute-start(bf16[64,64,128]{2,1,0:T(8,128)(2,1)S(1)} %get-tuple-element.22), channel_id=1, source_target_pairs={{0,6},{1,25},{2,0},{3,27},{4,2},{5,29},{6,4},{7,31},{8,14},{9,1},{... | collective-permute-start | bytes 3145736 | tf_op jit(solution)/shard_map/ppermute | solution.py:48
  78.3 0.6 copy-start.5
  78.9 1.0 copy-start.11
  79.9 18.4 %collective-permute-start.8 = (bf16[64,64,128]{2,1,0:T(8,128)(2,1)}, bf16[64,64,128]{2,1,0:T(8,128)(2,1)S(1)}, u32[]{:S(2)}, u32[]{:S(2)}) collective-permute-start(bf16[64,64,128]{2,1,0:T(8,128)(2,1)} %get-tuple-element.17), channel_id=1, source_target_pairs={{0,4},{1,17},{2,6},{3,19},{4,0},{5,21},{6,2},{7,23},{8,12},{9,25},... | collective-permute-start | bytes 3145736 | tf_op jit(solution)/shard_map/ppermute | solution.py:48
  79.9 1.0 copy-start.12
  80.9 26.9 %collective-permute-start.7 = (bf16[64,64,128]{2,1,0:T(8,128)(2,1)}, bf16[64,64,128]{2,1,0:T(8,128)(2,1)}, u32[]{:S(2)}, u32[]{:S(2)}) collective-permute-start(bf16[64,64,128]{2,1,0:T(8,128)(2,1)} %get-tuple-element.16), channel_id=1, source_target_pairs={{0,4},{1,17},{2,6},{3,19},{4,0},{5,21},{6,2},{7,23},{8,12},{9,25},... | collective-permute-start | bytes 3145736 | tf_op jit(solution)/shard_map/ppermute | solution.py:48
  84.5 0.6 copy-start.9
  84.5 23.3 %slice-start = ((s8[6291456]{0:T(1024)(128)(4,1)}), s8[4194304]{0:T(1024)(128)(4,1)S(1)}, s32[]{:S(2)}) async-start(s8[6291456]{0:T(1024)(128)(4,1)} %bitcast.34), calls=%async_computation.2 | async-start | bytes 8388608
  85.0 22.8 %slice-start.1 = ((s8[6291456]{0:T(1024)(128)(4,1)}), s8[2097152]{0:T(1024)(128)(4,1)S(1)}, s32[]{:S(2)}) async-start(s8[6291456]{0:T(1024)(128)(4,1)} %bitcast.34), calls=%async_computation.3 | async-start | bytes 4194304
  85.0 22.8 %copy-start.6 = (s32[40,128]{1,0:T(8,128)S(1)}, s32[40,128]{1,0:T(8,128)}, u32[]{:S(2)}) copy-start(s32[40,128]{1,0:T(8,128)} %copy-done.5) | copy-start | bytes 61444
  85.0 22.8 %copy-start.8 = (s32[4]{0:T(128)S(1)}, s32[4]{0:T(128)}, u32[]{:S(2)}) copy-start(s32[4]{0:T(128)} %pad_add_fusion.here.refs_0_.refs_1_) | copy-start | bytes 52
  107.8 0.8 copy-start.4
  108.6 0.7 copy-start.10
